TPU v7x, 32 devices: a whole 2x2x4 slice. The times are simulated.
32 devices in a mesh: dom: 16 (over z, y, x), depth: 2 (over core).
Axes of the slice: x: 2, y: 2, z: 4, core: 2. Of those that a mesh axis runs over, the one named last changes fastest.
Arguments:
- ancestors: int32 [16], P('dom'), may hold values from 0 to 15, as said below
- ensemble: float32 [16, 4, 12, 16, 128], P('dom', None, 'depth'), may hold values from -4 to 4
- diffusivity: float32 [12, 16, 128], P('depth'), may hold values from 0.02 to 0.1
- melting_speed: float32 [12, 16, 128], P('depth'), may hold values from 0.05 to 0.3
- permeability: float32 [12, 16, 128], P('depth'), may hold values from 0.5 to 2
Outputs:
- forecast_ensemble: float32 [16, 4, 12, 16, 128], P('dom', None, 'depth')
Inputs may be any that keep to these rules, and one draw needn't show every extreme that they name: `ancestors`: each entry names a particle; slots 0 and 2 descend from particle 1, slot 1 from particle 0, slot 3 from particle 16 - 1.
All inputs are finite; a program needn't handle non-finite values.
Results may differ from a plain program's by a relative error of at most 0.00002.
Values sent between devices are 32-bit elements; how exact they have to be, the bound alone decides.
No kernel may reach another device: no remote copies, remote signals or barrier semaphores. Data moves between devices by JAX's collectives and lax.ppermute only.
A program may use at most 64 MiB of HBM per device.

v0:
```python
import jax
import jax.numpy as jnp
from jax import lax
from jax.sharding import PartitionSpec as P

STEPS = 4


advect_coef = 0.1


def extended(block, sides, width):
    for axis, dim in sides:
        count = lax.axis_size(axis)
        forward = [(i, i + 1) for i in range(count - 1)]
        backward = [(target, source) for source, target in forward]
        low = lax.ppermute(
            lax.slice_in_dim(block, block.shape[dim] - width, None, axis=dim), axis, forward
        )
        high = lax.ppermute(lax.slice_in_dim(block, 0, width, axis=dim), axis, backward)
        block = jnp.concatenate([low, block, high], axis=dim)
    return block


def advance(padded, diffuse, reacts, permeab):
    center = padded[:, :, 1:-1]
    upper_cells = padded[:, :, :-2]
    lower_cells = padded[:, :, 2:]
    flat_pad = jnp.pad(center, ((0, 0), (0, 0), (0, 0), (1, 1), (1, 1)))
    laplacian_operator = (
        upper_cells + lower_cells + flat_pad[:, :, :, 2:, 1:-1] + flat_pad[:, :, :, :-2, 1:-1]
    )
    laplacian_operator = (
        laplacian_operator
        + flat_pad[:, :, :, 1:-1, 2:]
        + flat_pad[:, :, :, 1:-1, :-2]
        - 6.0 * center
    )
    velocity = center[:, 1]
    transport_update = advect_coef * jnp.maximum(velocity, 0.0)[:, None] * (center - upper_cells)
    transport_update = transport_update + advect_coef * jnp.minimum(velocity, 0.0)[:, None] * (
        lower_cells - center
    )
    fraction = center[:, 0]
    enthalpy = center[:, 2]
    composition = center[:, 3]
    melting = reacts * (enthalpy - 0.5 * composition)
    new_fraction = fraction - transport_update[:, 0] + melting
    new_velocity = (
        velocity + 0.2 * (permeab * jnp.tanh(fraction) - velocity) + 0.1 * laplacian_operator[:, 1]
    )
    new_enthalpy = (
        enthalpy - transport_update[:, 2] + diffuse * laplacian_operator[:, 2] - 0.5 * melting
    )
    new_composition = composition - transport_update[:, 3] + diffuse * laplacian_operator[:, 3]
    return jnp.stack([new_fraction, new_velocity, new_enthalpy, new_composition], axis=1)


def predict_forward(field_stack, diffusivity, melting_speed, permeability):

    def one_step(step_index, present_members):
        padded = extended(present_members, (("depth", 2),), 1)
        return advance(padded, diffusivity, melting_speed, permeability)

    return lax.fori_loop(0, STEPS, one_step, field_stack)


def local(ancestors, ensemble, diffusivity, melting_speed, permeability):
    source = ancestors[0]
    shard_rows = lax.all_gather(ensemble, "dom", axis=0, tiled=True)
    indices = jnp.arange(shard_rows.shape[0], dtype=jnp.int32)
    chosen = (indices == source).reshape((-1, 1, 1, 1, 1))
    present_members = jnp.sum(jnp.where(chosen, shard_rows, 0.0), axis=0, keepdims=True)
    return predict_forward(present_members, diffusivity, melting_speed, permeability)


def solution(mesh):
    return jax.shard_map(
        local,
        mesh=mesh,
        in_specs=(
            P("dom"),
            P("dom", None, "depth", None, None),
            P("depth", None, None),
            P("depth", None, None),
            P("depth", None, None),
        ),
        out_specs=P("dom", None, "depth", None, None),
        check_vma=False,
    )
```

profile of v0, /device:TPU:0, one launch (start us, length us, event | category | flops | bytes accessed | tf_op | source)
XLA Modules:
  0.0 112.7 jit_solution(18203314041827870242)
XLA Ops:
  6.5 0.7 all-gather.2.cloned.1.call-update
  7.9 73.1 %all-gather.2.cloned.1.call-done = f32[16,4,6,16,128]{4,3,2,1,0:T(8,128)} async-done(((f32[1,4,6,16,128]{4,3,2,1,0:T(8,128)}), f32[16,4,6,16,128]{4,3,2,1,0:T(8,128)}) %all-gather.2.cloned.1.call-update) | async-done | bytes 3145744 | tf_op jit(solution)/shard_map/all_gather | solution.py:70
  81.0 2.3 %select_reduce_fusion = f32[4,6,16,128]{3,2,1,0:T(8,128)S(1)} fusion(f32[16,4,6,16,128]{4,3,2,1,0:T(8,128)} %all-gather.2.cloned.1.call-done, pred[16]{0:T(512)(128)(4,1)S(1)} %iota_compare_fusion), kind=kLoop, calls=%fused_computation.36 | loop fusion | flops 1523712 | bytes 3342352 | tf_op jit(solution)/shard_map/reduce_sum | solution.py:73
  83.3 21.9 %while.12 = (s32[]{:T(128)}, f32[1,4,6,16,128]{4,3,2,1,0:T(8,128)S(1)}, f32[6,16,128]{2,1,0:T(8,128)S(1)}, f32[6,16,128]{2,1,0:T(8,128)S(1)}, f32[6,16,128]{2,1,0:T(8,128)S(1)}, /*index=5*/s32[]{:T(128)}) while((s32[]{:T(128)}, f32[1,4,6,16,128]{4,3,2,1,0:T(8,128)S(1)}, f32[6,16,128]{2,1,0:T(8,128)S(1)}, f32[6,16,128]{2,1,0:T(8,128)S(1)}, ...), condition=%wide.region_2.3_spmd, body=%wide.region_1.2_spmd.sunk | while | flops 1118210 | bytes 2523285 | solution.py:65
  83.3 1.3 %collective-permute-start = (f32[1,4,1,16,128]{4,3,2,1,0:T(8,128)S(1)}, f32[1,4,1,16,128]{4,3,2,1,0:T(8,128)S(1)}, u32[]{:S(2)}, u32[]{:S(2)}) collective-permute-start(f32[1,4,1,16,128]{4,3,2,1,0:T(8,128)S(1)} %get-tuple-element.132), channel_id=1, source_target_pairs={{1,0},{3,2},{5,4},{7,6},{9,8},{11,10},{13,12},{15,14},{17,16},{19,... | collective-permute-start | bytes 98312 | tf_op jit(solution)/shard_map/while/body/eval_jaxpr/ppermute | solution.py:20
  84.6 3.0 %collective-permute-start.1 = (f32[1,4,1,16,128]{4,3,2,1,0:T(8,128)S(1)}, f32[1,4,1,16,128]{4,3,2,1,0:T(8,128)S(1)}, u32[]{:S(2)}, u32[]{:S(2)}) collective-permute-start(f32[1,4,1,16,128]{4,3,2,1,0:T(8,128)S(1)} %get-tuple-element.133), channel_id=1, source_target_pairs={{0,1},{2,3},{4,5},{6,7},{8,9},{10,11},{12,13},{14,15},{16,17},{18,... | collective-permute-start | bytes 98312 | tf_op jit(solution)/shard_map/while/body/eval_jaxpr/ppermute | solution.py:17
  87.7 0.8 collective-permute-done.1
  88.5 0.2 fusion.24
  88.7 0.1 fusion.25
  88.8 1.3 %collective-permute-start = (f32[1,4,1,16,128]{4,3,2,1,0:T(8,128)S(1)}, f32[1,4,1,16,128]{4,3,2,1,0:T(8,128)S(1)}, u32[]{:S(2)}, u32[]{:S(2)}) collective-permute-start(f32[1,4,1,16,128]{4,3,2,1,0:T(8,128)S(1)} %get-tuple-element.132), channel_id=1, source_target_pairs={{1,0},{3,2},{5,4},{7,6},{9,8},{11,10},{13,12},{15,14},{17,16},{19,... | collective-permute-start | bytes 98312 | tf_op jit(solution)/shard_map/while/body/eval_jaxpr/ppermute | solution.py:20
  90.1 3.0 %collective-permute-start.1 = (f32[1,4,1,16,128]{4,3,2,1,0:T(8,128)S(1)}, f32[1,4,1,16,128]{4,3,2,1,0:T(8,128)S(1)}, u32[]{:S(2)}, u32[]{:S(2)}) collective-permute-start(f32[1,4,1,16,128]{4,3,2,1,0:T(8,128)S(1)} %get-tuple-element.133), channel_id=1, source_target_pairs={{0,1},{2,3},{4,5},{6,7},{8,9},{10,11},{12,13},{14,15},{16,17},{18,... | collective-permute-start | bytes 98312 | tf_op jit(solution)/shard_map/while/body/eval_jaxpr/ppermute | solution.py:17
  93.2 0.8 collective-permute-done.1
  94.0 0.2 fusion.24
  94.2 0.1 fusion.25
  94.3 1.3 %collective-permute-start = (f32[1,4,1,16,128]{4,3,2,1,0:T(8,128)S(1)}, f32[1,4,1,16,128]{4,3,2,1,0:T(8,128)S(1)}, u32[]{:S(2)}, u32[]{:S(2)}) collective-permute-start(f32[1,4,1,16,128]{4,3,2,1,0:T(8,128)S(1)} %get-tuple-element.132), channel_id=1, source_target_pairs={{1,0},{3,2},{5,4},{7,6},{9,8},{11,10},{13,12},{15,14},{17,16},{19,... | collective-permute-start | bytes 98312 | tf_op jit(solution)/shard_map/while/body/eval_jaxpr/ppermute | solution.py:20
  95.6 3.0 %collective-permute-start.1 = (f32[1,4,1,16,128]{4,3,2,1,0:T(8,128)S(1)}, f32[1,4,1,16,128]{4,3,2,1,0:T(8,128)S(1)}, u32[]{:S(2)}, u32[]{:S(2)}) collective-permute-start(f32[1,4,1,16,128]{4,3,2,1,0:T(8,128)S(1)} %get-tuple-element.133), channel_id=1, source_target_pairs={{0,1},{2,3},{4,5},{6,7},{8,9},{10,11},{12,13},{14,15},{16,17},{18,... | collective-permute-start | bytes 98312 | tf_op jit(solution)/shard_map/while/body/eval_jaxpr/ppermute | solution.py:17
  98.6 0.8 collective-permute-done.1
  99.4 0.2 fusion.24
  99.6 0.1 fusion.25
  99.7 1.3 %collective-permute-start = (f32[1,4,1,16,128]{4,3,2,1,0:T(8,128)S(1)}, f32[1,4,1,16,128]{4,3,2,1,0:T(8,128)S(1)}, u32[]{:S(2)}, u32[]{:S(2)}) collective-permute-start(f32[1,4,1,16,128]{4,3,2,1,0:T(8,128)S(1)} %get-tuple-element.132), channel_id=1, source_target_pairs={{1,0},{3,2},{5,4},{7,6},{9,8},{11,10},{13,12},{15,14},{17,16},{19,... | collective-permute-start | bytes 98312 | tf_op jit(solution)/shard_map/while/body/eval_jaxpr/ppermute | solution.py:20
  101.0 3.0 %collective-permute-start.1 = (f32[1,4,1,16,128]{4,3,2,1,0:T(8,128)S(1)}, f32[1,4,1,16,128]{4,3,2,1,0:T(8,128)S(1)}, u32[]{:S(2)}, u32[]{:S(2)}) collective-permute-start(f32[1,4,1,16,128]{4,3,2,1,0:T(8,128)S(1)} %get-tuple-element.133), channel_id=1, source_target_pairs={{0,1},{2,3},{4,5},{6,7},{8,9},{10,11},{12,13},{14,15},{16,17},{18,... | collective-permute-start | bytes 98312 | tf_op jit(solution)/shard_map/while/body/eval_jaxpr/ppermute | solution.py:17
  104.1 0.8 collective-permute-done.1
  104.9 0.2 fusion.24
  105.2 0.7 copy-done
  (26 shorter events, 0.2 us)
Async XLA Ops:
  6.5 76.7 %copy-start.1 = (f32[6,16,128]{2,1,0:T(8,128)S(1)}, f32[6,16,128]{2,1,0:T(8,128)}, u32[]{:S(2)}) copy-start(f32[6,16,128]{2,1,0:T(8,128)} %param.10) | copy-start | bytes 147460
  6.5 76.8 %copy-start.2 = (f32[6,16,128]{2,1,0:T(8,128)S(1)}, f32[6,16,128]{2,1,0:T(8,128)}, u32[]{:S(2)}) copy-start(f32[6,16,128]{2,1,0:T(8,128)} %param.11) | copy-start | bytes 147460
  6.5 76.8 %copy-start.3 = (f32[6,16,128]{2,1,0:T(8,128)S(1)}, f32[6,16,128]{2,1,0:T(8,128)}, u32[]{:S(2)}) copy-start(f32[6,16,128]{2,1,0:T(8,128)} %param.9) | copy-start | bytes 147460
  6.5 74.5 %all-gather.2.cloned.1.call-start = ((), (), s32[]{:S(2)}) async-start(), calls=%async_computation | async-start | bytes 3342336 | tf_op jit(solution)/shard_map/all_gather | solution.py:70
  83.3 4.4 %collective-permute-start = (f32[1,4,1,16,128]{4,3,2,1,0:T(8,128)S(1)}, f32[1,4,1,16,128]{4,3,2,1,0:T(8,128)S(1)}, u32[]{:S(2)}, u32[]{:S(2)}) collective-permute-start(f32[1,4,1,16,128]{4,3,2,1,0:T(8,128)S(1)} %get-tuple-element.132), channel_id=1, source_target_pairs={{1,0},{3,2},{5,4},{7,6},{9,8},{11,10},{13,12},{15,14},{17,16},{19,... | collective-permute-start | bytes 98312 | tf_op jit(solution)/shard_map/while/body/eval_jaxpr/ppermute | solution.py:20
  84.6 3.9 %collective-permute-start.1 = (f32[1,4,1,16,128]{4,3,2,1,0:T(8,128)S(1)}, f32[1,4,1,16,128]{4,3,2,1,0:T(8,128)S(1)}, u32[]{:S(2)}, u32[]{:S(2)}) collective-permute-start(f32[1,4,1,16,128]{4,3,2,1,0:T(8,128)S(1)} %get-tuple-element.133), channel_id=1, source_target_pairs={{0,1},{2,3},{4,5},{6,7},{8,9},{10,11},{12,13},{14,15},{16,17},{18,... | collective-permute-start | bytes 98312 | tf_op jit(solution)/shard_map/while/body/eval_jaxpr/ppermute | solution.py:17
  88.8 4.4 %collective-permute-start = (f32[1,4,1,16,128]{4,3,2,1,0:T(8,128)S(1)}, f32[1,4,1,16,128]{4,3,2,1,0:T(8,128)S(1)}, u32[]{:S(2)}, u32[]{:S(2)}) collective-permute-start(f32[1,4,1,16,128]{4,3,2,1,0:T(8,128)S(1)} %get-tuple-element.132), channel_id=1, source_target_pairs={{1,0},{3,2},{5,4},{7,6},{9,8},{11,10},{13,12},{15,14},{17,16},{19,... | collective-permute-start | bytes 98312 | tf_op jit(solution)/shard_map/while/body/eval_jaxpr/ppermute | solution.py:20
  90.1 3.9 %collective-permute-start.1 = (f32[1,4,1,16,128]{4,3,2,1,0:T(8,128)S(1)}, f32[1,4,1,16,128]{4,3,2,1,0:T(8,128)S(1)}, u32[]{:S(2)}, u32[]{:S(2)}) collective-permute-start(f32[1,4,1,16,128]{4,3,2,1,0:T(8,128)S(1)} %get-tuple-element.133), channel_id=1, source_target_pairs={{0,1},{2,3},{4,5},{6,7},{8,9},{10,11},{12,13},{14,15},{16,17},{18,... | collective-permute-start | bytes 98312 | tf_op jit(solution)/shard_map/while/body/eval_jaxpr/ppermute | solution.py:17
  94.3 4.4 %collective-permute-start = (f32[1,4,1,16,128]{4,3,2,1,0:T(8,128)S(1)}, f32[1,4,1,16,128]{4,3,2,1,0:T(8,128)S(1)}, u32[]{:S(2)}, u32[]{:S(2)}) collective-permute-start(f32[1,4,1,16,128]{4,3,2,1,0:T(8,128)S(1)} %get-tuple-element.132), channel_id=1, source_target_pairs={{1,0},{3,2},{5,4},{7,6},{9,8},{11,10},{13,12},{15,14},{17,16},{19,... | collective-permute-start | bytes 98312 | tf_op jit(solution)/shard_map/while/body/eval_jaxpr/ppermute | solution.py:20
  95.6 3.9 %collective-permute-start.1 = (f32[1,4,1,16,128]{4,3,2,1,0:T(8,128)S(1)}, f32[1,4,1,16,128]{4,3,2,1,0:T(8,128)S(1)}, u32[]{:S(2)}, u32[]{:S(2)}) collective-permute-start(f32[1,4,1,16,128]{4,3,2,1,0:T(8,128)S(1)} %get-tuple-element.133), channel_id=1, source_target_pairs={{0,1},{2,3},{4,5},{6,7},{8,9},{10,11},{12,13},{14,15},{16,17},{18,... | collective-permute-start | bytes 98312 | tf_op jit(solution)/shard_map/while/body/eval_jaxpr/ppermute | solution.py:17
  99.7 4.4 %collective-permute-start = (f32[1,4,1,16,128]{4,3,2,1,0:T(8,128)S(1)}, f32[1,4,1,16,128]{4,3,2,1,0:T(8,128)S(1)}, u32[]{:S(2)}, u32[]{:S(2)}) collective-permute-start(f32[1,4,1,16,128]{4,3,2,1,0:T(8,128)S(1)} %get-tuple-element.132), channel_id=1, source_target_pairs={{1,0},{3,2},{5,4},{7,6},{9,8},{11,10},{13,12},{15,14},{17,16},{19,... | collective-permute-start | bytes 98312 | tf_op jit(solution)/shard_map/while/body/eval_jaxpr/ppermute | solution.py:20
  101.0 3.9 %collective-permute-start.1 = (f32[1,4,1,16,128]{4,3,2,1,0:T(8,128)S(1)}, f32[1,4,1,16,128]{4,3,2,1,0:T(8,128)S(1)}, u32[]{:S(2)}, u32[]{:S(2)}) collective-permute-start(f32[1,4,1,16,128]{4,3,2,1,0:T(8,128)S(1)} %get-tuple-element.133), channel_id=1, source_target_pairs={{0,1},{2,3},{4,5},{6,7},{8,9},{10,11},{12,13},{14,15},{16,17},{18,... | collective-permute-start | bytes 98312 | tf_op jit(solution)/shard_map/while/body/eval_jaxpr/ppermute | solution.py:17
  105.2 0.7 copy-start
Sparse Core Ops, SparseCore 0:
  10.1 70.8 all-gather.1
where the time goes:
time: 113 us
  waiting for transfers between devices  77 us (68%)
  starting transfers between devices  17.3 us (15%)
  between operations  14.1 us (12%)
  other arithmetic  3.27 us (3%)
    all_gather x1, waiting for transfers between devices, local(): shard_rows = lax.all_gather(ensemble, 'dom', axis=0, tiled=True)  73.1 us
    ppermute x4, starting transfers between devices, extended(): lax.ppermute(lax.slice_in_dim(block, block.shape[dim] - width, None, axis...  12.1 us
    ppermute x4, starting transfers between devices, extended(): lax.ppermute(lax.slice_in_dim(block, 0, width, axis=dim), axis, backward)  5.17 us
    ppermute x4, waiting for transfers between devices, extended(): lax.ppermute(lax.slice_in_dim(block, block.shape[dim] - width, None, axis...  3.24 us
    reduce_sum x1, other arithmetic, local(): jnp.sum(jnp.where(chosen, shard_rows, 0.0), axis=0, keepdims=True)  2.27 us
  transfers between devices with their start and end apart: 9, of which 5 were waited for; matrix products, arithmetic and copies ran while one was open for 0% of the time, Pallas kernels for 0%

commit v1 on v0

v1 whole, which is shorter than its diff:
```python
import functools

import jax
import jax.numpy as jnp
from jax import lax
from jax.experimental import pallas as pl
from jax.experimental.pallas import tpu as pltpu
from jax.sharding import PartitionSpec as P

STEPS = 4
ADVECT = 0.1
SMEM = pl.BlockSpec(memory_space=pltpu.SMEM)
VMEM = pl.BlockSpec(memory_space=pltpu.VMEM)


def neighbours(q):
    rows = lax.broadcasted_iota(jnp.int32, q.shape, 0)
    columns = lax.broadcasted_iota(jnp.int32, q.shape, 1)
    high_row, high_column = q.shape[0] - 1, q.shape[1] - 1
    total = jnp.where(rows == 0, 0.0, pltpu.roll(q, 1, 0))
    total = total + jnp.where(rows == high_row, 0.0, pltpu.roll(q, high_row, 0))
    total = total + jnp.where(columns == 0, 0.0, pltpu.roll(q, 1, 1))
    return total + jnp.where(columns == high_column, 0.0, pltpu.roll(q, high_column, 1))


def layer_step(state, layer, diffuse, reacts, permeab):
    m, v, h, c = (state[q, layer] for q in range(4))
    m_up, v_up, h_up, c_up = (state[q, layer - 1] for q in range(4))
    m_low, v_low, h_low, c_low = (state[q, layer + 1] for q in range(4))
    down = ADVECT * jnp.maximum(v, 0.0)
    up = ADVECT * jnp.minimum(v, 0.0)

    def transport(q, upper, lower):
        return down * (q - upper) + up * (lower - q)

    def laplace(q, upper, lower):
        return upper + lower + neighbours(q) - 6.0 * q

    melting = reacts * (h - 0.5 * c)
    return (
        m - transport(m, m_up, m_low) + melting,
        v + 0.2 * (permeab * jnp.tanh(m) - v) + 0.1 * laplace(v, v_up, v_low),
        h - transport(h, h_up, h_low) + diffuse * laplace(h, h_up, h_low) - 0.5 * melting,
        c - transport(c, c_up, c_low) + diffuse * laplace(c, c_up, c_low),
    )


def forecast_kernel(
    cells, pair, place_ref, own, low, high, own_d, low_d, high_d, own_r, low_r, high_r, own_p, low_p, high_p,
    a_ref, b_ref, even, odd, coefs,
):
    place = place_ref[0]
    window = cells + (STEPS if pair else 2 * STEPS)
    zero = jnp.zeros(even.shape[2:], jnp.float32)
    for q in range(4):
        for buffer in (even, odd):
            buffer[q, 0] = zero
            buffer[q, window + 1] = zero

    def fill(at, start, source, first):
        for i in range(first[1]):
            for q in range(4):
                even[q, at + i] = source[0][0, q, start + i]
            for q in range(3):
                coefs[q, at + i] = source[1 + q][start + i]

    mine, lows, highs = (own, own_d, own_r, own_p), (low, low_d, low_r, low_p), (high, high_d, high_r, high_p)
    if pair:
        first = place == 0
        fill(jnp.where(first, 1, 1 + STEPS), 0, mine, (0, cells))
        fill(jnp.where(first, 1 + cells, 1), jnp.where(first, 0, cells - STEPS), lows, (0, STEPS))
    else:
        fill(1, cells - STEPS, lows, (0, STEPS))
        fill(1 + STEPS, 0, mine, (0, cells))
        fill(1 + STEPS + cells, 0, highs, (0, STEPS))
        inside_first = jnp.where(place == 0, 1 + STEPS, 0)
        inside_last = jnp.where(place == 2, STEPS + cells, window + 1)

    buffers = (even, odd)
    for step in range(STEPS):
        now, later = buffers[step % 2], buffers[1 - step % 2]
        left = STEPS - 1 - step
        if pair:
            start, count = jnp.where(first, 1, 2 + step), cells + left
        else:
            start, count = 2 + step, cells + 2 * left
        for i in range(count):
            layer = start + i
            values = layer_step(now, layer, coefs[0, layer], coefs[1, layer], coefs[2, layer])
            if step == STEPS - 1:
                a_ref[0, i], a_ref[1, i], b_ref[0, i], b_ref[1, i] = values
            else:
                for q in range(4):
                    value = values[q]
                    if not pair:
                        value = jnp.where((layer >= inside_first) & (layer <= inside_last), value, 0.0)
                    later[q, layer] = value


def forecast(ensemble, diffusivity, melting_speed, permeability):
    count = lax.axis_size("depth")
    arrays = (ensemble, diffusivity, melting_speed, permeability)
    pair = count == 2
    at = lax.axis_index("depth")
    if pair:
        swapped = [lax.ppermute(x, "depth", [(0, 1), (1, 0)]) for x in arrays]
        lows, highs, place = swapped, swapped, at
    else:
        up = [(i, i + 1) for i in range(count - 1)]
        lows = [lax.ppermute(x, "depth", up) for x in arrays]
        highs = [lax.ppermute(x, "depth", [(j, i) for i, j in up]) for x in arrays]
        place = jnp.where(at == 0, 0, jnp.where(at == count - 1, 2, 1))
    cells, rows, columns = diffusivity.shape
    window = cells + (STEPS if pair else 2 * STEPS)
    half = jax.ShapeDtypeStruct((2, cells, rows, columns), jnp.float32)
    operands = [x for group in zip(arrays, lows, highs) for x in group]
    return pl.pallas_call(
        functools.partial(forecast_kernel, cells, pair),
        out_shape=(half, half),
        in_specs=[SMEM] + [VMEM] * len(operands),
        out_specs=(VMEM, VMEM),
        scratch_shapes=[
            pltpu.VMEM((4, window + 2, rows, columns), jnp.float32),
            pltpu.VMEM((4, window + 2, rows, columns), jnp.float32),
            pltpu.VMEM((3, window + 2, rows, columns), jnp.float32),
        ],
        compiler_params=pltpu.CompilerParams(vmem_limit_bytes=16 * 1024 * 1024),
        name="forecast",
    )(place.reshape(1).astype(jnp.int32), *operands)


def choose_kernel(count, outputs, wanted, *refs):
    candidates, results = refs[:count], refs[count:]
    for j in range(outputs):
        for k in range(count):

            @pl.when(wanted[j] == k)
            def _(j=j, k=k):
                results[j][...] = candidates[k][...]


def choose(candidates, wanted, name):
    outputs = wanted.shape[0]
    one = jax.ShapeDtypeStruct(candidates[0].shape, jnp.float32)
    return pl.pallas_call(
        functools.partial(choose_kernel, len(candidates), outputs),
        out_shape=[one] * outputs,
        in_specs=[SMEM] + [VMEM] * len(candidates),
        out_specs=[VMEM] * outputs,
        compiler_params=pltpu.CompilerParams(vmem_limit_bytes=16 * 1024 * 1024),
        name=name,
    )(wanted, *candidates)


def finish_kernel(count, wanted, *refs):
    a_parts, b_parts, out = refs[:count], refs[count : -1], refs[-1]
    for k in range(count):

        @pl.when(wanted[0] == k)
        def _(k=k):
            out[0, 0:2] = a_parts[k][...]

    for k in range(len(b_parts)):

        @pl.when(wanted[1] == k)
        def _(k=k):
            out[0, 2:4] = b_parts[k][...]


def swap(x, distance):
    return lax.ppermute(x, "dom", [(i, i ^ distance) for i in range(lax.axis_size("dom"))])


def resample(ancestors, a, b):
    count = lax.axis_size("dom")
    me = lax.axis_index("dom")
    bits = count.bit_length() - 1
    inner = 1 << (bits // 2)
    outer = count // inner
    near, far = range(1, inner), range(1, outer)
    mine = ancestors.reshape(1)
    far_ancestors = [mine] + [swap(mine, j * inner) for j in far]
    near_ancestors = [mine] + [swap(mine, k) for k in near]
    b_got = [b] + [swap(b, j * inner) for j in far]
    a_got = [a] + [swap(a, k) for k in near]
    a_wanted = (jnp.concatenate(far_ancestors) ^ me) & (inner - 1)
    a_sent = choose(a_got, a_wanted, "choose_place")
    a_final = [a_sent[0]] + [swap(a_sent[j], j * inner) for j in far]
    b_wanted = (jnp.concatenate(near_ancestors) ^ me) // inner
    b_sent = choose(b_got, b_wanted, "choose_column")
    b_final = [b_sent[0]] + [swap(b_sent[k], k) for k in near]
    last = jnp.concatenate([(mine ^ me) // inner, (mine ^ me) & (inner - 1)])
    return pl.pallas_call(
        functools.partial(finish_kernel, outer),
        out_shape=jax.ShapeDtypeStruct((1, 4) + a.shape[1:], jnp.float32),
        in_specs=[SMEM] + [VMEM] * (outer + inner),
        out_specs=VMEM,
        compiler_params=pltpu.CompilerParams(vmem_limit_bytes=16 * 1024 * 1024),
        name="finish",
    )(last, *a_final, *b_final)


def local(ancestors, ensemble, diffusivity, melting_speed, permeability):
    a, b = forecast(ensemble, diffusivity, melting_speed, permeability)
    return resample(ancestors, a, b)


def solution(mesh):
    return jax.shard_map(
        local,
        mesh=mesh,
        in_specs=(
            P("dom"),
            P("dom", None, "depth", None, None),
            P("depth", None, None),
            P("depth", None, None),
            P("depth", None, None),
        ),
        out_specs=P("dom", None, "depth", None, None),
        check_vma=False,
    )
```

time: 113 us -> 42.6 us (0.38)
  waiting for transfers between devices: 77 us -> 4.54 us
  between operations: 14.1 us -> 0.79 us
  starting transfers between devices: 17.3 us -> 27 us
  Pallas kernels: 0 us -> 3.4 us
  local copies, waits for them, and re-layouts: 0.71 us -> 2.53 us
    all_gather x1 -> x0, waiting for transfers between devices: 73.1 us -> none  [local(): shard_rows = lax.all_gather(ensemble, 'dom', axis=0, tiled=True)]
    ppermute x8 -> x22, starting transfers between devices: 17.3 us -> 27 us  [the longest x18 26 us: swap(): lax.ppermute(x, 'dom', [(i, i ^ distance) for i in range(lax.axis_size('d...]
    pallas_call x0 -> x4, Pallas kernels: none -> 3.4 us  [the longest x2 1.36 us: choose(): pl.pallas_call(functools.partial(choose_kernel, len(candidates), outputs)...]
    reduce_sum x1 -> x0, other arithmetic: 2.27 us -> none  [local(): jnp.sum(jnp.where(chosen, shard_rows, 0.0), axis=0, keepdims=True)]
    select_n x0 -> x1, other arithmetic: none -> 2.01 us  [resample(): b_wanted = (jnp.concatenate(near_ancestors) ^ me) // inner]
    and x0 -> x1, other arithmetic: none -> 1.94 us  [resample(): a_wanted = (jnp.concatenate(far_ancestors) ^ me) & inner - 1]
    unnamed x8, local copies, waits for them, and re-layouts: 0.68 us -> 2.53 us
    ppermute x8 -> x22, waiting for transfers between devices: 3.25 us -> 4.54 us  [the longest x18 4.53 us: swap(): lax.ppermute(x, 'dom', [(i, i ^ distance) for i in range(lax.axis_size('d...]
  transfers between devices with their start and end apart: 9 -> 22, of which waited for: 5 -> 6; matrix products, arithmetic and copies ran while one was open for 0% -> 10% of each run, Pallas kernels for 0% -> 5%
where the time goes in v1:
time: 42.6 us; the launch traced here: 42.3 us
  starting transfers between devices  27 us (63%)
  waiting for transfers between devices  4.54 us (11%)
  other arithmetic  4.03 us (9%)
  Pallas kernels  3.4 us (8%)
  local copies, waits for them, and re-layouts  2.53 us (6%)
  between operations  0.79 us (2%)
    ppermute x18, starting transfers between devices, swap(): lax.ppermute(x, 'dom', [(i, i ^ distance) for i in range(lax.axis_size('d...  26 us
    ppermute x18, waiting for transfers between devices, swap(): lax.ppermute(x, 'dom', [(i, i ^ distance) for i in range(lax.axis_size('d...  4.53 us
    unnamed x8, local copies, waits for them, and re-layouts  2.53 us
    select_n x1, other arithmetic, resample(): b_wanted = (jnp.concatenate(near_ancestors) ^ me) // inner  2.01 us
    and x1, other arithmetic, resample(): a_wanted = (jnp.concatenate(far_ancestors) ^ me) & inner - 1  1.94 us
    pallas_call x2, Pallas kernels, choose(): pl.pallas_call(functools.partial(choose_kernel, len(candidates), outputs)...  1.36 us
    pallas_call x1, Pallas kernels, resample(): pl.pallas_call(functools.partial(finish_kernel, outer), out_shape=jax.Sha...  1.29 us
    ppermute x4, starting transfers between devices, forecast(): swapped = [lax.ppermute(x, 'depth', [(0, 1), (1, 0)]) for x in arrays]  1.03 us
  transfers between devices with their start and end apart: 22, of which 6 were waited for; matrix products, arithmetic and copies ran while one was open for 10% of the time, Pallas kernels for 5%

profile of v1, /device:TPU:0, one launch (start us, length us, event | category | flops | bytes accessed | tf_op | source)
XLA Modules:
  0.0 42.3 jit_solution(12124096819288540700)
XLA Ops:
  1.0 2.9 %collective-permute-start.13 = (s32[1]{0:T(128)}, s32[1]{0:T(128)}, u32[]{:S(2)}, u32[]{:S(2)}) collective-permute-start(s32[1]{0:T(128)} %param.5), channel_id=1, source_target_pairs={{0,2},{2,0},{4,6},{6,4},{8,10},{10,8},{12,14},{14,12},{16,18},{18,... | collective-permute-start | bytes 20 | tf_op jit(solution)/shard_map/ppermute | solution.py:171
  4.7 3.7 %collective-permute-start.2 = (s32[1]{0:T(128)}, s32[1]{0:T(128)}, u32[]{:S(2)}, u32[]{:S(2)}) collective-permute-start(s32[1]{0:T(128)} %param.5), channel_id=1, source_target_pairs={{0,24},{2,26},{4,28},{6,30},{8,16},{10,18},{12,20},{14,22},{16,8},... | collective-permute-start | bytes 20 | tf_op jit(solution)/shard_map/ppermute | solution.py:171
  8.4 0.8 %collective-permute-start = (s32[1]{0:T(128)}, s32[1]{0:T(128)}, u32[]{:S(2)}, u32[]{:S(2)}) collective-permute-start(s32[1]{0:T(128)} %param.5), channel_id=1, source_target_pairs={{0,8},{2,10},{4,12},{6,14},{8,0},{10,2},{12,4},{14,6},{16,24},{18,... | collective-permute-start | bytes 20 | tf_op jit(solution)/shard_map/ppermute | solution.py:171
  9.2 1.5 %collective-permute-start.14 = (s32[1]{0:T(128)}, s32[1]{0:T(128)}, u32[]{:S(2)}, u32[]{:S(2)}) collective-permute-start(s32[1]{0:T(128)} %param.5), channel_id=1, source_target_pairs={{0,4},{2,6},{4,0},{6,2},{8,12},{10,14},{12,8},{14,10},{16,20},{18,... | collective-permute-start | bytes 20 | tf_op jit(solution)/shard_map/ppermute | solution.py:171
  10.7 0.9 %copy-done = f32[1,4,6,16,128]{4,3,2,1,0:T(8,128)S(1)} copy-done((f32[1,4,6,16,128]{4,3,2,1,0:T(8,128)S(1)}, f32[1,4,6,16,128]{4,3,2,1,0:T(8,128)}, u32[]{:S(2)}) %copy-start) | copy-done | bytes 196632
  11.6 0.8 %copy-done.2 = f32[6,16,128]{2,1,0:T(8,128)S(1)} copy-done((f32[6,16,128]{2,1,0:T(8,128)S(1)}, f32[6,16,128]{2,1,0:T(8,128)}, u32[]{:S(2)}) %copy-start.2) | copy-done | bytes 49176
  12.4 0.8 %copy-done.3 = f32[6,16,128]{2,1,0:T(8,128)S(1)} copy-done((f32[6,16,128]{2,1,0:T(8,128)S(1)}, f32[6,16,128]{2,1,0:T(8,128)}, u32[]{:S(2)}) %copy-start.3) | copy-done | bytes 49176
  13.2 0.8 %forecast.1 = (f32[2,6,16,128]{3,2,1,0:T(8,128)S(1)}, f32[2,6,16,128]{3,2,1,0:T(8,128)S(1)}) custom-call(s32[1]{0:T(128)} %bitcast.1.place_ref, f32[1,4,6,16,128]{4,3,2,1,0:T(8,128)S(1)} %copy-done, f32[1,4,6,16,128]{4,3,2,1,0:T(8,128)S(1)} %collective-permute-done.3.low.high, f32[1,4,6,16,128]{4,3,2,1,0:T(8,128)S(1)} %collective-permute-done.3.low.high, ...), custom_call_target="tpu_custom_call" | custom-call | tf_op jit(solution)/shard_map/forecast/pallas_call | solution.py:117
  14.4 1.7 %collective-permute-start.8 = (f32[2,6,16,128]{3,2,1,0:T(8,128)S(1)}, f32[2,6,16,128]{3,2,1,0:T(8,128)S(1)}, u32[]{:S(2)}, u32[]{:S(2)}) collective-permute-start(f32[2,6,16,128]{3,2,1,0:T(8,128)S(1)} %get-tuple-element.15.refs_0_), channel_id=1, source_target_pairs={{0,4},{2,6},{4,0},{6,2},{8,12},{10,14},{12,8},{14,10},{16,20},{18,... | collective-permute-start | bytes 294920 | tf_op jit(solution)/shard_map/ppermute | solution.py:171
  16.0 1.5 %collective-permute-start.7 = (f32[2,6,16,128]{3,2,1,0:T(8,128)S(1)}, f32[2,6,16,128]{3,2,1,0:T(8,128)S(1)}, u32[]{:S(2)}, u32[]{:S(2)}) collective-permute-start(f32[2,6,16,128]{3,2,1,0:T(8,128)S(1)} %get-tuple-element.15.refs_0_), channel_id=1, source_target_pairs={{0,2},{2,0},{4,6},{6,4},{8,10},{10,8},{12,14},{14,12},{16,18},{18,... | collective-permute-start | bytes 294920 | tf_op jit(solution)/shard_map/ppermute | solution.py:171
  17.5 1.9 %fusion.wanted = s32[4]{0:T(128)S(1)} fusion(s32[1]{0:T(128)} %collective-permute-done.2, s32[1]{0:T(128)} %collective-permute-done.1, s32[1]{0:T(128)} %collective-permute-done, s32[1]{0:T(128)S(6)} %copy.6, s32[]{:T(128)} %axis_index.23), kind=kLoop, calls=%fused_computation.6 | loop fusion | flops 20 | bytes 36 | tf_op jit(solution)/shard_map/and | solution.py:186
  19.7 0.9 %collective-permute-start.15 = (s32[1]{0:T(128)}, s32[1]{0:T(128)}, u32[]{:S(2)}, u32[]{:S(2)}) collective-permute-start(s32[1]{0:T(128)} %param.5), channel_id=1, source_target_pairs={{0,6},{2,4},{4,2},{6,0},{8,14},{10,12},{12,10},{14,8},{16,22},{18,... | collective-permute-start | bytes 20 | tf_op jit(solution)/shard_map/ppermute | solution.py:171
  20.6 3.9 %collective-permute-start.18 = (f32[2,6,16,128]{3,2,1,0:T(8,128)S(1)}, f32[2,6,16,128]{3,2,1,0:T(8,128)S(1)}, u32[]{:S(2)}, u32[]{:S(2)}) collective-permute-start(f32[2,6,16,128]{3,2,1,0:T(8,128)S(1)} %get-tuple-element.20.refs_0_), channel_id=1, source_target_pairs={{0,24},{2,26},{4,28},{6,30},{8,16},{10,18},{12,20},{14,22},{16,8},... | collective-permute-start | bytes 294920 | tf_op jit(solution)/shard_map/ppermute | solution.py:171
  24.6 0.7 %choose_place.1 = (f32[2,6,16,128]{3,2,1,0:T(8,128)S(1)}, f32[2,6,16,128]{3,2,1,0:T(8,128)S(1)}, f32[2,6,16,128]{3,2,1,0:T(8,128)S(1)}, f32[2,6,16,128]{3,2,1,0:T(8,128)S(1)}) custom-call(s32[4]{0:T(128)S(1)} %fusion.wanted, f32[2,6,16,128]{3,2,1,0:T(8,128)S(1)} %get-tuple-element.15.refs_0_, f32[2,6,16,128]{3,2,1,0:T(8,128)S(1)} %collective-permute-done.7.refs_1_, ...), custom_call_target="tpu_custom_call" | custom-call | tf_op jit(solution)/shard_map/choose_place/pallas_call | solution.py:145
  25.2 0.7 %collective-permute-start.16 = (f32[2,6,16,128]{3,2,1,0:T(8,128)S(1)}, f32[2,6,16,128]{3,2,1,0:T(8,128)S(1)}, u32[]{:S(2)}, u32[]{:S(2)}) collective-permute-start(f32[2,6,16,128]{3,2,1,0:T(8,128)S(1)} %get-tuple-element.20.refs_0_), channel_id=1, source_target_pairs={{0,8},{2,10},{4,12},{6,14},{8,0},{10,2},{12,4},{14,6},{16,24},{18,... | collective-permute-start | bytes 294920 | tf_op jit(solution)/shard_map/ppermute | solution.py:171
  25.9 1.4 %collective-permute-start.10 = (f32[2,6,16,128]{3,2,1,0:T(8,128)S(1)}, f32[2,6,16,128]{3,2,1,0:T(8,128)S(1)}, u32[]{:S(2)}, u32[]{:S(2)}) collective-permute-start(f32[2,6,16,128]{3,2,1,0:T(8,128)S(1)} %get-tuple-element.17), channel_id=1, source_target_pairs={{0,8},{2,10},{4,12},{6,14},{8,0},{10,2},{12,4},{14,6},{16,24},{18,... | collective-permute-start | bytes 294920 | tf_op jit(solution)/shard_map/ppermute | solution.py:171
  27.3 2.0 %and_select_fusion.wanted = s32[4]{0:T(128)S(1)} fusion(s32[1]{0:T(128)} %collective-permute-done.15, s32[1]{0:T(128)} %collective-permute-done.14, s32[1]{0:T(128)} %collective-permute-done.13, s32[1]{0:T(128)S(6)} %copy.6, s32[]{:T(128)} %axis_index.23), kind=kLoop, calls=%fused_computation | loop fusion | flops 76 | bytes 36 | tf_op jit(solution)/shard_map/jit(floor_divide)/jit(_where)/select_n | solution.py:189
  29.4 3.0 %collective-permute-start.11 = (f32[2,6,16,128]{3,2,1,0:T(8,128)S(1)}, f32[2,6,16,128]{3,2,1,0:T(8,128)S(1)}, u32[]{:S(2)}, u32[]{:S(2)}) collective-permute-start(f32[2,6,16,128]{3,2,1,0:T(8,128)S(1)} %get-tuple-element.18), channel_id=1, source_target_pairs={{0,16},{2,18},{4,20},{6,22},{8,24},{10,26},{12,28},{14,30},{16,0},... | collective-permute-start | bytes 294920 | tf_op jit(solution)/shard_map/ppermute | solution.py:171
  32.4 1.3 %collective-permute-done.17.refs_2_ = f32[2,6,16,128]{3,2,1,0:T(8,128)S(1)} collective-permute-done((f32[2,6,16,128]{3,2,1,0:T(8,128)S(1)}, f32[2,6,16,128]{3,2,1,0:T(8,128)S(1)}, u32[]{:S(2)}, u32[]{:S(2)}) %collective-permute-start.17) | collective-permute-done | bytes 98336 | tf_op jit(solution)/shard_map/ppermute | solution.py:171
  34.6 0.9 %collective-permute-start.20 = (f32[2,6,16,128]{3,2,1,0:T(8,128)S(1)}, f32[2,6,16,128]{3,2,1,0:T(8,128)S(1)}, u32[]{:S(2)}, u32[]{:S(2)}) collective-permute-start(f32[2,6,16,128]{3,2,1,0:T(8,128)S(1)} %get-tuple-element.23), channel_id=1, source_target_pairs={{0,4},{2,6},{4,0},{6,2},{8,12},{10,14},{12,8},{14,10},{16,20},{18,... | collective-permute-start | bytes 294920 | tf_op jit(solution)/shard_map/ppermute | solution.py:171
  35.5 2.4 %collective-permute-start.21 = (f32[2,6,16,128]{3,2,1,0:T(8,128)S(1)}, f32[2,6,16,128]{3,2,1,0:T(8,128)S(1)}, u32[]{:S(2)}, u32[]{:S(2)}) collective-permute-start(f32[2,6,16,128]{3,2,1,0:T(8,128)S(1)} %get-tuple-element.24), channel_id=1, source_target_pairs={{0,6},{2,4},{4,2},{6,0},{8,14},{10,12},{12,10},{14,8},{16,22},{18,... | collective-permute-start | bytes 294920 | tf_op jit(solution)/shard_map/ppermute | solution.py:171
  38.0 0.8 %collective-permute-done.12.refs_3_ = f32[2,6,16,128]{3,2,1,0:T(8,128)S(1)} collective-permute-done((f32[2,6,16,128]{3,2,1,0:T(8,128)S(1)}, f32[2,6,16,128]{3,2,1,0:T(8,128)S(1)}, u32[]{:S(2)}, u32[]{:S(2)}) %collective-permute-start.12) | collective-permute-done | bytes 98336 | tf_op jit(solution)/shard_map/ppermute | solution.py:171
  39.2 1.9 %collective-permute-done.21.refs_7_ = f32[2,6,16,128]{3,2,1,0:T(8,128)S(1)} collective-permute-done((f32[2,6,16,128]{3,2,1,0:T(8,128)S(1)}, f32[2,6,16,128]{3,2,1,0:T(8,128)S(1)}, u32[]{:S(2)}, u32[]{:S(2)}) %collective-permute-start.21) | collective-permute-done | bytes 98336 | tf_op jit(solution)/shard_map/ppermute | solution.py:171
  41.0 1.3 %finish.1 = f32[1,4,6,16,128]{4,3,2,1,0:T(8,128)} custom-call(s32[2]{0:T(128)S(1)} %pad_add_fusion.wanted, f32[2,6,16,128]{3,2,1,0:T(8,128)S(1)} %get-tuple-element.16.refs_0_, f32[2,6,16,128]{3,2,1,0:T(8,128)S(1)} %collective-permute-done.10.refs_1_, f32[2,6,16,128]{3,2,1,0:T(8,128)S(1)} %collective-permute-done.11.refs_2_, ...), custom_call_target="tpu_custom_call" | custom-call | tf_op jit(solution)/shard_map/finish/pallas_call | solution.py:193
  (35 shorter events, 3.0 us)
Async XLA Ops:
  0.0 10.7 %copy-start.1 = (f32[6,16,128]{2,1,0:T(8,128)S(1)}, f32[6,16,128]{2,1,0:T(8,128)}, u32[]{:S(2)}) copy-start(f32[6,16,128]{2,1,0:T(8,128)} %own_d.1) | copy-start | bytes 147460
  0.0 9.1 %collective-permute-start.3 = (f32[1,4,6,16,128]{4,3,2,1,0:T(8,128)}, f32[1,4,6,16,128]{4,3,2,1,0:T(8,128)S(1)}, u32[]{:S(2)}, u32[]{:S(2)}) collective-permute-start(f32[1,4,6,16,128]{4,3,2,1,0:T(8,128)} %own.1), channel_id=1, source_target_pairs={{0,1},{1,0},{2,3},{3,2},{4,5},{5,4},{6,7},{7,6},{8,9},{9,8},{10,11... | collective-permute-start | bytes 589832 | tf_op jit(solution)/shard_map/ppermute | solution.py:106
  0.5 4.2 %collective-permute-start.4 = (f32[6,16,128]{2,1,0:T(8,128)}, f32[6,16,128]{2,1,0:T(8,128)S(1)}, u32[]{:S(2)}, u32[]{:S(2)}) collective-permute-start(f32[6,16,128]{2,1,0:T(8,128)} %own_d.1), channel_id=1, source_target_pairs={{0,1},{1,0},{2,3},{3,2},{4,5},{5,4},{6,7},{7,6},{8,9},{9,8},{10,11... | collective-permute-start | bytes 147464 | tf_op jit(solution)/shard_map/ppermute | solution.py:106
  0.5 7.8 %collective-permute-start.5 = (f32[6,16,128]{2,1,0:T(8,128)}, f32[6,16,128]{2,1,0:T(8,128)S(1)}, u32[]{:S(2)}, u32[]{:S(2)}) collective-permute-start(f32[6,16,128]{2,1,0:T(8,128)} %own_r.1), channel_id=1, source_target_pairs={{0,1},{1,0},{2,3},{3,2},{4,5},{5,4},{6,7},{7,6},{8,9},{9,8},{10,11... | collective-permute-start | bytes 147464 | tf_op jit(solution)/shard_map/ppermute | solution.py:106
  1.0 7.4 %collective-permute-start.6 = (f32[6,16,128]{2,1,0:T(8,128)}, f32[6,16,128]{2,1,0:T(8,128)S(1)}, u32[]{:S(2)}, u32[]{:S(2)}) collective-permute-start(f32[6,16,128]{2,1,0:T(8,128)} %own_p.1), channel_id=1, source_target_pairs={{0,1},{1,0},{2,3},{3,2},{4,5},{5,4},{6,7},{7,6},{8,9},{9,8},{10,11... | collective-permute-start | bytes 147464 | tf_op jit(solution)/shard_map/ppermute | solution.py:106
  1.0 24.2 %collective-permute-start.13 = (s32[1]{0:T(128)}, s32[1]{0:T(128)}, u32[]{:S(2)}, u32[]{:S(2)}) collective-permute-start(s32[1]{0:T(128)} %param.5), channel_id=1, source_target_pairs={{0,2},{2,0},{4,6},{6,4},{8,10},{10,8},{12,14},{14,12},{16,18},{18,... | collective-permute-start | bytes 20 | tf_op jit(solution)/shard_map/ppermute | solution.py:171
  4.7 9.3 %collective-permute-start.2 = (s32[1]{0:T(128)}, s32[1]{0:T(128)}, u32[]{:S(2)}, u32[]{:S(2)}) collective-permute-start(s32[1]{0:T(128)} %param.5), channel_id=1, source_target_pairs={{0,24},{2,26},{4,28},{6,30},{8,16},{10,18},{12,20},{14,22},{16,8},... | collective-permute-start | bytes 20 | tf_op jit(solution)/shard_map/ppermute | solution.py:171
  8.4 6.0 %collective-permute-start.1 = (s32[1]{0:T(128)}, s32[1]{0:T(128)}, u32[]{:S(2)}, u32[]{:S(2)}) collective-permute-start(s32[1]{0:T(128)} %param.5), channel_id=1, source_target_pairs={{0,16},{2,18},{4,20},{6,22},{8,24},{10,26},{12,28},{14,30},{16,0},... | collective-permute-start | bytes 20 | tf_op jit(solution)/shard_map/ppermute | solution.py:171
  8.4 7.7 %collective-permute-start = (s32[1]{0:T(128)}, s32[1]{0:T(128)}, u32[]{:S(2)}, u32[]{:S(2)}) collective-permute-start(s32[1]{0:T(128)} %param.5), channel_id=1, source_target_pairs={{0,8},{2,10},{4,12},{6,14},{8,0},{10,2},{12,4},{14,6},{16,24},{18,... | collective-permute-start | bytes 20 | tf_op jit(solution)/shard_map/ppermute | solution.py:171
  9.2 16.8 %collective-permute-start.14 = (s32[1]{0:T(128)}, s32[1]{0:T(128)}, u32[]{:S(2)}, u32[]{:S(2)}) collective-permute-start(s32[1]{0:T(128)} %param.5), channel_id=1, source_target_pairs={{0,4},{2,6},{4,0},{6,2},{8,12},{10,14},{12,8},{14,10},{16,20},{18,... | collective-permute-start | bytes 20 | tf_op jit(solution)/shard_map/ppermute | solution.py:171
  10.7 0.9 %copy-start = (f32[1,4,6,16,128]{4,3,2,1,0:T(8,128)S(1)}, f32[1,4,6,16,128]{4,3,2,1,0:T(8,128)}, u32[]{:S(2)}) copy-start(f32[1,4,6,16,128]{4,3,2,1,0:T(8,128)} %own.1) | copy-start | bytes 589828
  14.0 5.7 %collective-permute-start.9 = (f32[2,6,16,128]{3,2,1,0:T(8,128)S(1)}, f32[2,6,16,128]{3,2,1,0:T(8,128)S(1)}, u32[]{:S(2)}, u32[]{:S(2)}) collective-permute-start(f32[2,6,16,128]{3,2,1,0:T(8,128)S(1)} %get-tuple-element.15.refs_0_), channel_id=1, source_target_pairs={{0,6},{2,4},{4,2},{6,0},{8,14},{10,12},{12,10},{14,8},{16,22},{18,... | collective-permute-start | bytes 294920 | tf_op jit(solution)/shard_map/ppermute | solution.py:171
  14.4 6.2 %collective-permute-start.8 = (f32[2,6,16,128]{3,2,1,0:T(8,128)S(1)}, f32[2,6,16,128]{3,2,1,0:T(8,128)S(1)}, u32[]{:S(2)}, u32[]{:S(2)}) collective-permute-start(f32[2,6,16,128]{3,2,1,0:T(8,128)S(1)} %get-tuple-element.15.refs_0_), channel_id=1, source_target_pairs={{0,4},{2,6},{4,0},{6,2},{8,12},{10,14},{12,8},{14,10},{16,20},{18,... | collective-permute-start | bytes 294920 | tf_op jit(solution)/shard_map/ppermute | solution.py:171
  16.0 8.5 %collective-permute-start.7 = (f32[2,6,16,128]{3,2,1,0:T(8,128)S(1)}, f32[2,6,16,128]{3,2,1,0:T(8,128)S(1)}, u32[]{:S(2)}, u32[]{:S(2)}) collective-permute-start(f32[2,6,16,128]{3,2,1,0:T(8,128)S(1)} %get-tuple-element.15.refs_0_), channel_id=1, source_target_pairs={{0,2},{2,0},{4,6},{6,4},{8,10},{10,8},{12,14},{14,12},{16,18},{18,... | collective-permute-start | bytes 294920 | tf_op jit(solution)/shard_map/ppermute | solution.py:171
  19.7 7.7 %collective-permute-start.15 = (s32[1]{0:T(128)}, s32[1]{0:T(128)}, u32[]{:S(2)}, u32[]{:S(2)}) collective-permute-start(s32[1]{0:T(128)} %param.5), channel_id=1, source_target_pairs={{0,6},{2,4},{4,2},{6,0},{8,14},{10,12},{12,10},{14,8},{16,22},{18,... | collective-permute-start | bytes 20 | tf_op jit(solution)/shard_map/ppermute | solution.py:171
  20.6 11.7 %collective-permute-start.18 = (f32[2,6,16,128]{3,2,1,0:T(8,128)S(1)}, f32[2,6,16,128]{3,2,1,0:T(8,128)S(1)}, u32[]{:S(2)}, u32[]{:S(2)}) collective-permute-start(f32[2,6,16,128]{3,2,1,0:T(8,128)S(1)} %get-tuple-element.20.refs_0_), channel_id=1, source_target_pairs={{0,24},{2,26},{4,28},{6,30},{8,16},{10,18},{12,20},{14,22},{16,8},... | collective-permute-start | bytes 294920 | tf_op jit(solution)/shard_map/ppermute | solution.py:171
  24.5 9.1 %collective-permute-start.17 = (f32[2,6,16,128]{3,2,1,0:T(8,128)S(1)}, f32[2,6,16,128]{3,2,1,0:T(8,128)S(1)}, u32[]{:S(2)}, u32[]{:S(2)}) collective-permute-start(f32[2,6,16,128]{3,2,1,0:T(8,128)S(1)} %get-tuple-element.20.refs_0_), channel_id=1, source_target_pairs={{0,16},{2,18},{4,20},{6,22},{8,24},{10,26},{12,28},{14,30},{16,0},... | collective-permute-start | bytes 294920 | tf_op jit(solution)/shard_map/ppermute | solution.py:171
  25.2 8.4 %collective-permute-start.16 = (f32[2,6,16,128]{3,2,1,0:T(8,128)S(1)}, f32[2,6,16,128]{3,2,1,0:T(8,128)S(1)}, u32[]{:S(2)}, u32[]{:S(2)}) collective-permute-start(f32[2,6,16,128]{3,2,1,0:T(8,128)S(1)} %get-tuple-element.20.refs_0_), channel_id=1, source_target_pairs={{0,8},{2,10},{4,12},{6,14},{8,0},{10,2},{12,4},{14,6},{16,24},{18,... | collective-permute-start | bytes 294920 | tf_op jit(solution)/shard_map/ppermute | solution.py:171
  25.9 9.6 %collective-permute-start.10 = (f32[2,6,16,128]{3,2,1,0:T(8,128)S(1)}, f32[2,6,16,128]{3,2,1,0:T(8,128)S(1)}, u32[]{:S(2)}, u32[]{:S(2)}) collective-permute-start(f32[2,6,16,128]{3,2,1,0:T(8,128)S(1)} %get-tuple-element.17), channel_id=1, source_target_pairs={{0,8},{2,10},{4,12},{6,14},{8,0},{10,2},{12,4},{14,6},{16,24},{18,... | collective-permute-start | bytes 294920 | tf_op jit(solution)/shard_map/ppermute | solution.py:171
  29.4 8.7 %collective-permute-start.11 = (f32[2,6,16,128]{3,2,1,0:T(8,128)S(1)}, f32[2,6,16,128]{3,2,1,0:T(8,128)S(1)}, u32[]{:S(2)}, u32[]{:S(2)}) collective-permute-start(f32[2,6,16,128]{3,2,1,0:T(8,128)S(1)} %get-tuple-element.18), channel_id=1, source_target_pairs={{0,16},{2,18},{4,20},{6,22},{8,24},{10,26},{12,28},{14,30},{16,0},... | collective-permute-start | bytes 294920 | tf_op jit(solution)/shard_map/ppermute | solution.py:171
  32.3 6.5 %collective-permute-start.12 = (f32[2,6,16,128]{3,2,1,0:T(8,128)S(1)}, f32[2,6,16,128]{3,2,1,0:T(8,128)S(1)}, u32[]{:S(2)}, u32[]{:S(2)}) collective-permute-start(f32[2,6,16,128]{3,2,1,0:T(8,128)S(1)} %get-tuple-element.19), channel_id=1, source_target_pairs={{0,24},{2,26},{4,28},{6,30},{8,16},{10,18},{12,20},{14,22},{16,8},... | collective-permute-start | bytes 294920 | tf_op jit(solution)/shard_map/ppermute | solution.py:171
  34.4 4.7 %collective-permute-start.19 = (f32[2,6,16,128]{3,2,1,0:T(8,128)S(1)}, f32[2,6,16,128]{3,2,1,0:T(8,128)S(1)}, u32[]{:S(2)}, u32[]{:S(2)}) collective-permute-start(f32[2,6,16,128]{3,2,1,0:T(8,128)S(1)} %get-tuple-element.22), channel_id=1, source_target_pairs={{0,2},{2,0},{4,6},{6,4},{8,10},{10,8},{12,14},{14,12},{16,18},{18,... | collective-permute-start | bytes 294920 | tf_op jit(solution)/shard_map/ppermute | solution.py:171
  34.6 4.6 %collective-permute-start.20 = (f32[2,6,16,128]{3,2,1,0:T(8,128)S(1)}, f32[2,6,16,128]{3,2,1,0:T(8,128)S(1)}, u32[]{:S(2)}, u32[]{:S(2)}) collective-permute-start(f32[2,6,16,128]{3,2,1,0:T(8,128)S(1)} %get-tuple-element.23), channel_id=1, source_target_pairs={{0,4},{2,6},{4,0},{6,2},{8,12},{10,14},{12,8},{14,10},{16,20},{18,... | collective-permute-start | bytes 294920 | tf_op jit(solution)/shard_map/ppermute | solution.py:171
  35.5 5.5 %collective-permute-start.21 = (f32[2,6,16,128]{3,2,1,0:T(8,128)S(1)}, f32[2,6,16,128]{3,2,1,0:T(8,128)S(1)}, u32[]{:S(2)}, u32[]{:S(2)}) collective-permute-start(f32[2,6,16,128]{3,2,1,0:T(8,128)S(1)} %get-tuple-element.24), channel_id=1, source_target_pairs={{0,6},{2,4},{4,2},{6,0},{8,14},{10,12},{12,10},{14,8},{16,22},{18,... | collective-permute-start | bytes 294920 | tf_op jit(solution)/shard_map/ppermute | solution.py:171
  (2 other events, 1.6 us)

commit v2 on v1

v2 whole, which is shorter than its diff:
```python
import functools

import jax
import jax.numpy as jnp
from jax import lax
from jax.experimental import pallas as pl
from jax.experimental.pallas import tpu as pltpu
from jax.sharding import PartitionSpec as P

STEPS = 4
ORDER = (1, 2, 3), (1, 2, 3)
ADVECT = 0.1
SMEM = pl.BlockSpec(memory_space=pltpu.SMEM)
VMEM = pl.BlockSpec(memory_space=pltpu.VMEM)
LIMIT = pltpu.CompilerParams(vmem_limit_bytes=32 * 1024 * 1024)


def neighbours(q):
    rows = lax.broadcasted_iota(jnp.int32, q.shape, 0)
    columns = lax.broadcasted_iota(jnp.int32, q.shape, 1)
    high_row, high_column = q.shape[0] - 1, q.shape[1] - 1
    total = jnp.where(rows == 0, 0.0, pltpu.roll(q, 1, 0))
    total = total + jnp.where(rows == high_row, 0.0, pltpu.roll(q, high_row, 0))
    total = total + jnp.where(columns == 0, 0.0, pltpu.roll(q, 1, 1))
    return total + jnp.where(columns == high_column, 0.0, pltpu.roll(q, high_column, 1))


def layer_step(state, layer, diffuse, reacts, permeab):
    m, v, h, c = (state[q, layer] for q in range(4))
    m_up, v_up, h_up, c_up = (state[q, layer - 1] for q in range(4))
    m_low, v_low, h_low, c_low = (state[q, layer + 1] for q in range(4))
    down = ADVECT * jnp.maximum(v, 0.0)
    up = ADVECT * jnp.minimum(v, 0.0)

    def transport(q, upper, lower):
        return down * (q - upper) + up * (lower - q)

    def laplace(q, upper, lower):
        return upper + lower + neighbours(q) - 6.0 * q

    melting = reacts * (h - 0.5 * c)
    return (
        m - transport(m, m_up, m_low) + melting,
        v + 0.2 * (permeab * jnp.tanh(m) - v) + 0.1 * laplace(v, v_up, v_low),
        h - transport(h, h_up, h_low) + diffuse * laplace(h, h_up, h_low) - 0.5 * melting,
        c - transport(c, c_up, c_low) + diffuse * laplace(c, c_up, c_low),
    )


def forecast_kernel(cells, pair, count, *refs):
    own, own_coefs, low, high = refs[0], refs[1:4], refs[4], refs[5]
    out, even, odd, coefs = refs[6:]
    at = lax.axis_index("depth")
    window = cells + (STEPS if pair else 2 * STEPS)
    zero = jnp.zeros(even.shape[2:], jnp.float32)
    for q in range(4):
        for buffer in (even, odd):
            buffer[q, 0] = zero
            buffer[q, window + 1] = zero

    def fill(to, layers, state):
        for i in range(layers):
            for q in range(7):
                (even if q < 4 else coefs)[q % 4, to + i] = state(q, i)

    def mine(q, i):
        return own[0, q, i] if q < 4 else own_coefs[q - 4][i]

    if pair:
        first = at == 0
        fill(jnp.where(first, 1, 1 + STEPS), cells, mine)
        fill(jnp.where(first, 1 + cells, 1), STEPS, lambda q, i: low[q, i])
    else:
        fill(1, STEPS, lambda q, i: low[q, i])
        fill(1 + STEPS, cells, mine)
        fill(1 + STEPS + cells, STEPS, lambda q, i: high[q, i])
        inside_first = jnp.where(at == 0, 1 + STEPS, 0)
        inside_last = jnp.where(at == count - 1, STEPS + cells, window + 1)

    buffers = (even, odd)
    for step in range(STEPS):
        now, later = buffers[step % 2], buffers[1 - step % 2]
        left = STEPS - 1 - step
        if pair:
            start, layers = jnp.where(first, 1, 2 + step), cells + left
        else:
            start, layers = 2 + step, cells + 2 * left
        for i in range(layers):
            layer = start + i
            values = layer_step(now, layer, coefs[0, layer], coefs[1, layer], coefs[2, layer])
            for q in range(4):
                value = values[q]
                if step == STEPS - 1:
                    out[0, q, i] = value
                    continue
                if not pair:
                    value = jnp.where((layer >= inside_first) & (layer <= inside_last), value, 0.0)
                later[q, layer] = value


def other_side(x, towards):
    count = lax.axis_size("depth")
    if count == 2:
        return lax.ppermute(x, "depth", [(0, 1), (1, 0)])
    return lax.ppermute(x, "depth", [(i, i + towards) for i in range(count) if 0 <= i + towards < count])


def forecast(state, edges, coefs):
    count = lax.axis_size("depth")
    pair = count == 2
    _, _, cells, rows, columns = state.shape
    window = cells + (STEPS if pair else 2 * STEPS)
    if pair:
        low = high = other_side(edges[0], 1)
    else:
        low, high = other_side(edges[1], 1), other_side(edges[0], -1)
    return pl.pallas_call(
        functools.partial(forecast_kernel, cells, pair, count),
        out_shape=jax.ShapeDtypeStruct(state.shape, jnp.float32),
        in_specs=[VMEM] * 6,
        out_specs=VMEM,
        scratch_shapes=[
            pltpu.VMEM((4, window + 2, rows, columns), jnp.float32),
            pltpu.VMEM((4, window + 2, rows, columns), jnp.float32),
            pltpu.VMEM((3, window + 2, rows, columns), jnp.float32),
        ],
        compiler_params=LIMIT,
        name="forecast",
    )(state, *coefs, low, high)


def first_wishes_kernel(mine, other, out):
    rows = lax.broadcasted_iota(jnp.int32, out.shape, 0)
    pair = [jnp.broadcast_to(x[...].reshape(1, 1), out.shape) for x in (mine, other)]
    out[...] = jnp.where(rows == 0, pair[0], pair[1])


def join_wishes_kernel(known, mine, other, out):
    rows = lax.broadcasted_iota(jnp.int32, out.shape, 0)
    out[...] = jnp.where(rows < known, mine[...], pltpu.roll(other[...], known, 0))


def hop(wish, sides, phase):
    offset = wish ^ lax.axis_index("dom")
    inner = offset & (sides - 1)
    outer = lax.shift_right_logical(offset, sides.bit_length() - 1)
    return jnp.where(lax.axis_index("depth") % 2 == phase, inner, outer)


def tiles(shape):
    return [(0, q, i, slice(r, r + 8)) for q in range(shape[1]) for i in range(shape[2]) for r in range(0, shape[3], 8)]


def pick(values, masks):
    value = values[0]
    for mask, other in zip(masks, values[1:]):
        value = jnp.where(mask, other, value)
    return value


def masks_of(wish, sides, phase):
    wanted = jnp.broadcast_to(hop(wish, sides, phase), (8, wish.shape[-1]))
    return [wanted == k for k in range(1, sides)]


def near_kernel(sides, wishes, state, out):
    out[...] = hop(wishes[...], sides, 0)


def choose_kernel(sides, *refs):
    candidates, near, far, results = refs[:sides], refs[sides], refs[sides + 1], refs[sides + 2 :]
    half = sides // 2
    wanted = near[...], hop(far[...], sides, 0)
    masks = [
        [jnp.broadcast_to(wanted[j // half][j % half : j % half + 1], near.shape) == k for k in range(1, sides)]
        for j in range(sides)
    ]
    for at in tiles(candidates[0].shape):
        values = [candidate[at] for candidate in candidates]
        for j in range(sides):
            results[j][at] = pick(values, masks[j])


def settle_kernel(sides, pair, *refs):
    candidates, wishes, coefs = refs[:sides], refs[sides], refs[sides + 1 : sides + 4]
    result, edges = refs[sides + 4], refs[sides + 5 :]
    masks = masks_of(wishes[0:1], sides, 1)
    for at in tiles(result.shape):
        result[at] = pick([candidate[at] for candidate in candidates], masks)
    cells = result.shape[2]
    starts = [jnp.where(lax.axis_index("depth") == 0, cells - STEPS, 0)] if pair else [0, cells - STEPS]
    for start, edge in zip(starts, edges):
        for q in range(4):
            edge[q] = result[0, q, pl.ds(start, STEPS)]
        for q in range(3):
            edge[4 + q] = coefs[q][pl.ds(start, STEPS)]


def swap(x, distance, phase):
    count, depth = lax.axis_size("dom"), lax.axis_size("depth")
    sides = 1 << (count.bit_length() // 2)
    pairs = []
    for i in range(count):
        for d in range(depth):
            pairs.append((i * depth + d, (i ^ (distance if d % 2 == phase else distance * sides)) * depth + d))
    return lax.ppermute(x, ("dom", "depth"), pairs)


def local(ancestors, ensemble, diffusivity, melting_speed, permeability):
    count, depth = lax.axis_size("dom"), lax.axis_size("depth")
    sides = 1 << (count.bit_length() // 2)
    assert sides * sides == count
    far = range(1, sides)
    like = jax.ShapeDtypeStruct(ensemble.shape, jnp.float32)
    other = swap(ancestors, 1, 1)
    first, second = ORDER if sides == 4 else (far, far)
    got = {k: swap(ensemble, k, 0) for k in first}
    coefs = (diffusivity, melting_speed, permeability)
    wishes = pl.pallas_call(
        first_wishes_kernel,
        out_shape=jax.ShapeDtypeStruct((8, ensemble.shape[-1]), jnp.int32),
        in_specs=[VMEM] * 2,
        out_specs=VMEM,
        compiler_params=LIMIT,
        name="first_wishes",
    )(ancestors, other)
    known = 2
    while 2 * known < sides:
        wishes = pl.pallas_call(
            functools.partial(join_wishes_kernel, known),
            out_shape=jax.ShapeDtypeStruct(wishes.shape, jnp.int32),
            in_specs=[VMEM] * 2,
            out_specs=VMEM,
            compiler_params=LIMIT,
            name="join_wishes",
        )(wishes, swap(wishes, known, 1))
        known *= 2
    far_wishes = swap(wishes, known, 1)
    near = pl.pallas_call(
        functools.partial(near_kernel, sides),
        out_shape=jax.ShapeDtypeStruct(wishes.shape, jnp.int32),
        in_specs=[VMEM] * 2,
        out_specs=VMEM,
        compiler_params=LIMIT,
        name="near",
    )(wishes, ensemble)
    sent = pl.pallas_call(
        functools.partial(choose_kernel, sides),
        out_shape=[like] * sides,
        in_specs=[VMEM] * (sides + 2),
        out_specs=[VMEM] * sides,
        compiler_params=LIMIT,
        name="choose",
    )(ensemble, *(got[k] for k in far), near, far_wishes)
    final = {k: swap(sent[k], k, 1) for k in second}
    edge = jax.ShapeDtypeStruct((7, STEPS) + ensemble.shape[3:], jnp.float32)
    edges = [edge] if depth == 2 else [edge, edge]
    state, *edges = pl.pallas_call(
        functools.partial(settle_kernel, sides, depth == 2),
        out_shape=[like] + edges,
        in_specs=[VMEM] * (sides + 4),
        out_specs=[VMEM] * (1 + len(edges)),
        compiler_params=LIMIT,
        name="settle",
    )(sent[0], *(final[k] for k in far), wishes, *coefs)
    return forecast(state, edges, coefs)


def solution(mesh):
    return jax.shard_map(
        local,
        mesh=mesh,
        in_specs=(
            P("dom"),
            P("dom", None, "depth", None, None),
            P("depth", None, None),
            P("depth", None, None),
            P("depth", None, None),
        ),
        out_specs=P("dom", None, "depth", None, None),
        check_vma=False,
    )
```

time: 42.6 us -> 29.7 us (0.70)
  starting transfers between devices: 27 us -> 14.1 us
  waiting for transfers between devices: 4.54 us -> 11.2 us
  other arithmetic: 4.03 us -> 0 us
  local copies, waits for them, and re-layouts: 2.53 us -> 1.14 us
  Pallas kernels: 3.4 us -> 2.31 us
    ppermute x22 -> x9, starting transfers between devices: 27 us -> 14.1 us  [the longest x8 14 us: swap(): return lax.ppermute(x, ('dom', 'depth'), pairs)]
    ppermute x22 -> x9, waiting for transfers between devices: 4.54 us -> 11.2 us  [the longest x8 9.72 us: swap(): return lax.ppermute(x, ('dom', 'depth'), pairs)]
    select_n x1 -> x0, other arithmetic: 2.01 us -> none  [resample(): b_wanted = (jnp.concatenate(near_ancestors) ^ me) // inner]
    and x1 -> x0, other arithmetic: 1.94 us -> none  [resample(): a_wanted = (jnp.concatenate(far_ancestors) ^ me) & inner - 1]
    unnamed x8 -> x10, local copies, waits for them, and re-layouts: 2.53 us -> 1.14 us
    pallas_call x4 -> x5, Pallas kernels: 3.4 us -> 2.31 us  [the longest x1 1.44 us: forecast(): pl.pallas_call(functools.partial(forecast_kernel, cells, pair, count), ou...]
  transfers between devices with their start and end apart: 22 -> 9, of which waited for: 6 -> 5; matrix products, arithmetic and copies ran while one was open for 10% -> 0% of each run, Pallas kernels for 5% -> 2%
where the time goes in v2:
time: 29.7 us; the launch traced here: 29.5 us
  starting transfers between devices  14.1 us (47%)
  waiting for transfers between devices  11.2 us (38%)
  Pallas kernels  2.31 us (8%)
  local copies, waits for them, and re-layouts  1.14 us (4%)
  between operations  0.75 us (3%)
    ppermute x8, starting transfers between devices, swap(): return lax.ppermute(x, ('dom', 'depth'), pairs)  14 us
    ppermute x8, waiting for transfers between devices, swap(): return lax.ppermute(x, ('dom', 'depth'), pairs)  9.72 us
    ppermute x1, waiting for transfers between devices, other_side(): return lax.ppermute(x, 'depth', [(0, 1), (1, 0)])  1.48 us
    pallas_call x1, Pallas kernels, forecast(): pl.pallas_call(functools.partial(forecast_kernel, cells, pair, count), ou...  1.44 us
    unnamed x10, local copies, waits for them, and re-layouts  1.14 us
    pallas_call x1, Pallas kernels, local(): pl.pallas_call(first_wishes_kernel, out_shape=jax.ShapeDtypeStruct((8, en...  0.69 us
  transfers between devices with their start and end apart: 9, of which 5 were waited for; matrix products, arithmetic and copies ran while one was open for 0% of the time, Pallas kernels for 2%

profile of v2, /device:TPU:0, one launch (start us, length us, event | category | flops | bytes accessed | tf_op | source)
XLA Modules:
  0.0 29.5 jit_solution(10284354512692660530)
XLA Ops:
  0.0 3.9 %collective-permute-start.2 = (f32[1,4,6,16,128]{4,3,2,1,0:T(8,128)}, f32[1,4,6,16,128]{4,3,2,1,0:T(8,128)S(1)}, u32[]{:S(2)}, u32[]{:S(2)}) collective-permute-start(f32[1,4,6,16,128]{4,3,2,1,0:T(8,128)} %refs_0_.1), channel_id=1, source_target_pairs={{0,6},{1,25},{2,4},{3,27},{4,2},{5,29},{6,0},{7,31},{8,14},{9,17},... | collective-permute-start | bytes 589832 | tf_op jit(solution)/shard_map/ppermute | solution.py:206
  3.9 0.5 %collective-permute-start.1 = (f32[1,4,6,16,128]{4,3,2,1,0:T(8,128)}, f32[1,4,6,16,128]{4,3,2,1,0:T(8,128)S(1)}, u32[]{:S(2)}, u32[]{:S(2)}) collective-permute-start(f32[1,4,6,16,128]{4,3,2,1,0:T(8,128)} %refs_0_.1), channel_id=1, source_target_pairs={{0,4},{1,17},{2,6},{3,19},{4,0},{5,21},{6,2},{7,23},{8,12},{9,25},... | collective-permute-start | bytes 589832 | tf_op jit(solution)/shard_map/ppermute | solution.py:206
  4.4 0.1 collective-permute-start
  4.5 2.1 %collective-permute-start.3 = (s32[1]{0:T(128)}, s32[1]{0:T(128)}, u32[]{:S(2)}, u32[]{:S(2)}) collective-permute-start(s32[1]{0:T(128)} %param.5), channel_id=1, source_target_pairs={{0,8},{1,3},{2,10},{3,1},{4,12},{5,7},{6,14},{7,5},{8,0},{9,11},{1... | collective-permute-start | bytes 20 | tf_op jit(solution)/shard_map/ppermute | solution.py:206
  7.2 1.0 %collective-permute-done.3.other = s32[1]{0:T(128)} collective-permute-done((s32[1]{0:T(128)}, s32[1]{0:T(128)}, u32[]{:S(2)}, u32[]{:S(2)}) %collective-permute-start.3) | collective-permute-done | bytes 36 | tf_op jit(solution)/shard_map/ppermute | solution.py:206
  8.2 0.7 %first_wishes.1.wishes.refs_4_ = s32[8,128]{1,0:T(8,128)S(1)} custom-call(s32[1]{0:T(128)S(6)} %copy.6.mine, s32[1]{0:T(128)} %collective-permute-done.3.other), custom_call_target="tpu_custom_call" | custom-call | tf_op jit(solution)/shard_map/first_wishes/pallas_call | solution.py:219
  8.9 3.1 %collective-permute-start.4 = (s32[8,128]{1,0:T(8,128)S(1)}, s32[8,128]{1,0:T(8,128)S(1)}, u32[]{:S(2)}, u32[]{:S(2)}) collective-permute-start(s32[8,128]{1,0:T(8,128)S(1)} %first_wishes.1.wishes.refs_4_), channel_id=1, source_target_pairs={{0,16},{1,5},{2,18},{3,7},{4,20},{5,1},{6,22},{7,3},{8,24},{9,13},... | collective-permute-start | bytes 12296 | tf_op jit(solution)/shard_map/ppermute | solution.py:206
  11.9 0.9 %copy-done = f32[1,4,6,16,128]{4,3,2,1,0:T(8,128)S(1)} copy-done((f32[1,4,6,16,128]{4,3,2,1,0:T(8,128)S(1)}, f32[1,4,6,16,128]{4,3,2,1,0:T(8,128)}, u32[]{:S(2)}) %copy-start) | copy-done | bytes 196632
  12.9 0.0 copy-start.3
  12.9 0.0 copy-start.4
  12.9 0.7 %collective-permute-done.4.refs_5_ = s32[8,128]{1,0:T(8,128)S(1)} collective-permute-done((s32[8,128]{1,0:T(8,128)S(1)}, s32[8,128]{1,0:T(8,128)S(1)}, u32[]{:S(2)}, u32[]{:S(2)}) %collective-permute-start.4) | collective-permute-done | bytes 4128 | tf_op jit(solution)/shard_map/ppermute | solution.py:206
  13.6 0.0 collective-permute-done.refs_1_
  13.6 0.2 copy-done.1
  13.8 0.1 choose.1
  13.9 1.7 %collective-permute-start.5 = (f32[1,4,6,16,128]{4,3,2,1,0:T(8,128)S(1)}, f32[1,4,6,16,128]{4,3,2,1,0:T(8,128)S(1)}, u32[]{:S(2)}, u32[]{:S(2)}) collective-permute-start(f32[1,4,6,16,128]{4,3,2,1,0:T(8,128)S(1)} %get-tuple-element.12), channel_id=1, source_target_pairs={{0,8},{1,3},{2,10},{3,1},{4,12},{5,7},{6,14},{7,5},{8,0},{9,11},{1... | collective-permute-start | bytes 589832 | tf_op jit(solution)/shard_map/ppermute | solution.py:206
  15.6 2.6 %collective-permute-start.6 = (f32[1,4,6,16,128]{4,3,2,1,0:T(8,128)S(1)}, f32[1,4,6,16,128]{4,3,2,1,0:T(8,128)S(1)}, u32[]{:S(2)}, u32[]{:S(2)}) collective-permute-start(f32[1,4,6,16,128]{4,3,2,1,0:T(8,128)S(1)} %get-tuple-element.13), channel_id=1, source_target_pairs={{0,16},{1,5},{2,18},{3,7},{4,20},{5,1},{6,22},{7,3},{8,24},{9,13},... | collective-permute-start | bytes 589832 | tf_op jit(solution)/shard_map/ppermute | solution.py:206
  18.2 0.1 collective-permute-start.7
  18.3 1.3 %collective-permute-done.5.refs_1_ = f32[1,4,6,16,128]{4,3,2,1,0:T(8,128)S(1)} collective-permute-done((f32[1,4,6,16,128]{4,3,2,1,0:T(8,128)S(1)}, f32[1,4,6,16,128]{4,3,2,1,0:T(8,128)S(1)}, u32[]{:S(2)}, u32[]{:S(2)}) %collective-permute-start.5) | collective-permute-done | bytes 196640 | tf_op jit(solution)/shard_map/ppermute | solution.py:206
  19.6 6.8 %collective-permute-done.6.refs_2_ = f32[1,4,6,16,128]{4,3,2,1,0:T(8,128)S(1)} collective-permute-done((f32[1,4,6,16,128]{4,3,2,1,0:T(8,128)S(1)}, f32[1,4,6,16,128]{4,3,2,1,0:T(8,128)S(1)}, u32[]{:S(2)}, u32[]{:S(2)}) %collective-permute-start.6) | collective-permute-done | bytes 196640 | tf_op jit(solution)/shard_map/ppermute | solution.py:206
  26.4 0.0 collective-permute-done.7.refs_3_
  26.4 0.1 settle.1
  26.5 0.1 collective-permute-start.8
  26.6 1.5 %collective-permute-done.8.refs_4_.refs_5_ = f32[7,4,16,128]{3,2,1,0:T(8,128)S(1)} collective-permute-done((f32[7,4,16,128]{3,2,1,0:T(8,128)S(1)}, f32[7,4,16,128]{3,2,1,0:T(8,128)S(1)}, u32[]{:S(2)}, u32[]{:S(2)}) %collective-permute-start.8) | collective-permute-done | bytes 229408 | tf_op jit(solution)/shard_map/ppermute | solution.py:104
  28.0 1.4 %forecast.1 = f32[1,4,6,16,128]{4,3,2,1,0:T(8,128)} custom-call(f32[1,4,6,16,128]{4,3,2,1,0:T(8,128)S(1)} %get-tuple-element.15.refs_0_, f32[6,16,128]{2,1,0:T(8,128)S(1)} %copy-done.2, f32[6,16,128]{2,1,0:T(8,128)S(1)} %copy-done.3, f32[6,16,128]{2,1,0:T(8,128)S(1)} %copy-done.4, f32[7,4,16,128]{3,2,1,0:T(8,128)S(1)} %collective-permute-done.8.refs_4_.refs_5_, ...), custom_call_target="tpu_custom_call" | custom-call | tf_op jit(solution)/shard_map/forecast/pallas_call | solution.py:117
  (9 shorter events, 0.0 us)
Async XLA Ops:
  0.0 13.6 %collective-permute-start.2 = (f32[1,4,6,16,128]{4,3,2,1,0:T(8,128)}, f32[1,4,6,16,128]{4,3,2,1,0:T(8,128)S(1)}, u32[]{:S(2)}, u32[]{:S(2)}) collective-permute-start(f32[1,4,6,16,128]{4,3,2,1,0:T(8,128)} %refs_0_.1), channel_id=1, source_target_pairs={{0,6},{1,25},{2,4},{3,27},{4,2},{5,29},{6,0},{7,31},{8,14},{9,17},... | collective-permute-start | bytes 589832 | tf_op jit(solution)/shard_map/ppermute | solution.py:206
  3.9 9.7 %collective-permute-start.1 = (f32[1,4,6,16,128]{4,3,2,1,0:T(8,128)}, f32[1,4,6,16,128]{4,3,2,1,0:T(8,128)S(1)}, u32[]{:S(2)}, u32[]{:S(2)}) collective-permute-start(f32[1,4,6,16,128]{4,3,2,1,0:T(8,128)} %refs_0_.1), channel_id=1, source_target_pairs={{0,4},{1,17},{2,6},{3,19},{4,0},{5,21},{6,2},{7,23},{8,12},{9,25},... | collective-permute-start | bytes 589832 | tf_op jit(solution)/shard_map/ppermute | solution.py:206
  4.4 9.2 %collective-permute-start = (f32[1,4,6,16,128]{4,3,2,1,0:T(8,128)}, f32[1,4,6,16,128]{4,3,2,1,0:T(8,128)S(1)}, u32[]{:S(2)}, u32[]{:S(2)}) collective-permute-start(f32[1,4,6,16,128]{4,3,2,1,0:T(8,128)} %refs_0_.1), channel_id=1, source_target_pairs={{0,2},{1,9},{2,0},{3,11},{4,6},{5,13},{6,4},{7,15},{8,10},{9,1},{1... | collective-permute-start | bytes 589832 | tf_op jit(solution)/shard_map/ppermute | solution.py:206
  4.5 3.7 %collective-permute-start.3 = (s32[1]{0:T(128)}, s32[1]{0:T(128)}, u32[]{:S(2)}, u32[]{:S(2)}) collective-permute-start(s32[1]{0:T(128)} %param.5), channel_id=1, source_target_pairs={{0,8},{1,3},{2,10},{3,1},{4,12},{5,7},{6,14},{7,5},{8,0},{9,11},{1... | collective-permute-start | bytes 20 | tf_op jit(solution)/shard_map/ppermute | solution.py:206
  8.9 4.7 %collective-permute-start.4 = (s32[8,128]{1,0:T(8,128)S(1)}, s32[8,128]{1,0:T(8,128)S(1)}, u32[]{:S(2)}, u32[]{:S(2)}) collective-permute-start(s32[8,128]{1,0:T(8,128)S(1)} %first_wishes.1.wishes.refs_4_), channel_id=1, source_target_pairs={{0,16},{1,5},{2,18},{3,7},{4,20},{5,1},{6,22},{7,3},{8,24},{9,13},... | collective-permute-start | bytes 12296 | tf_op jit(solution)/shard_map/ppermute | solution.py:206
  11.9 0.9 %copy-start = (f32[1,4,6,16,128]{4,3,2,1,0:T(8,128)S(1)}, f32[1,4,6,16,128]{4,3,2,1,0:T(8,128)}, u32[]{:S(2)}) copy-start(f32[1,4,6,16,128]{4,3,2,1,0:T(8,128)} %refs_0_.1) | copy-start | bytes 589828
  12.8 0.9 %copy-start.1 = (f32[1,4,6,16,128]{4,3,2,1,0:T(8,128)S(1)}, f32[1,4,6,16,128]{4,3,2,1,0:T(8,128)}, u32[]{:S(2)}) copy-start(f32[1,4,6,16,128]{4,3,2,1,0:T(8,128)} %refs_0_.1) | copy-start | bytes 589828
  12.9 13.5 %copy-start.2 = (f32[6,16,128]{2,1,0:T(8,128)S(1)}, f32[6,16,128]{2,1,0:T(8,128)}, u32[]{:S(2)}) copy-start(f32[6,16,128]{2,1,0:T(8,128)} %refs_1_.1) | copy-start | bytes 147460
  12.9 13.5 %copy-start.3 = (f32[6,16,128]{2,1,0:T(8,128)S(1)}, f32[6,16,128]{2,1,0:T(8,128)}, u32[]{:S(2)}) copy-start(f32[6,16,128]{2,1,0:T(8,128)} %refs_2_.1) | copy-start | bytes 147460
  12.9 13.5 %copy-start.4 = (f32[6,16,128]{2,1,0:T(8,128)S(1)}, f32[6,16,128]{2,1,0:T(8,128)}, u32[]{:S(2)}) copy-start(f32[6,16,128]{2,1,0:T(8,128)} %refs_3_.1) | copy-start | bytes 147460
  13.9 5.7 %collective-permute-start.5 = (f32[1,4,6,16,128]{4,3,2,1,0:T(8,128)S(1)}, f32[1,4,6,16,128]{4,3,2,1,0:T(8,128)S(1)}, u32[]{:S(2)}, u32[]{:S(2)}) collective-permute-start(f32[1,4,6,16,128]{4,3,2,1,0:T(8,128)S(1)} %get-tuple-element.12), channel_id=1, source_target_pairs={{0,8},{1,3},{2,10},{3,1},{4,12},{5,7},{6,14},{7,5},{8,0},{9,11},{1... | collective-permute-start | bytes 589832 | tf_op jit(solution)/shard_map/ppermute | solution.py:206
  15.6 10.8 %collective-permute-start.6 = (f32[1,4,6,16,128]{4,3,2,1,0:T(8,128)S(1)}, f32[1,4,6,16,128]{4,3,2,1,0:T(8,128)S(1)}, u32[]{:S(2)}, u32[]{:S(2)}) collective-permute-start(f32[1,4,6,16,128]{4,3,2,1,0:T(8,128)S(1)} %get-tuple-element.13), channel_id=1, source_target_pairs={{0,16},{1,5},{2,18},{3,7},{4,20},{5,1},{6,22},{7,3},{8,24},{9,13},... | collective-permute-start | bytes 589832 | tf_op jit(solution)/shard_map/ppermute | solution.py:206
  18.2 8.2 %collective-permute-start.7 = (f32[1,4,6,16,128]{4,3,2,1,0:T(8,128)S(1)}, f32[1,4,6,16,128]{4,3,2,1,0:T(8,128)S(1)}, u32[]{:S(2)}, u32[]{:S(2)}) collective-permute-start(f32[1,4,6,16,128]{4,3,2,1,0:T(8,128)S(1)} %get-tuple-element.14), channel_id=1, source_target_pairs={{0,24},{1,7},{2,26},{3,5},{4,28},{5,3},{6,30},{7,1},{8,16},{9,15},... | collective-permute-start | bytes 589832 | tf_op jit(solution)/shard_map/ppermute | solution.py:206
  26.5 1.6 %collective-permute-start.8 = (f32[7,4,16,128]{3,2,1,0:T(8,128)S(1)}, f32[7,4,16,128]{3,2,1,0:T(8,128)S(1)}, u32[]{:S(2)}, u32[]{:S(2)}) collective-permute-start(f32[7,4,16,128]{3,2,1,0:T(8,128)S(1)} %get-tuple-element.16), channel_id=1, source_target_pairs={{0,1},{1,0},{2,3},{3,2},{4,5},{5,4},{6,7},{7,6},{8,9},{9,8},{10,11... | collective-permute-start | bytes 688136 | tf_op jit(solution)/shard_map/ppermute | solution.py:104

commit v3 on v2

--- a/solution.py
+++ b/solution.py
@@ -1,4 +1,6 @@
 import functools
+import itertools
+import operator
 
 import jax
 import jax.numpy as jnp
@@ -8,10 +10,10 @@
 from jax.sharding import PartitionSpec as P
 
 STEPS = 4
-ORDER = (1, 2, 3), (1, 2, 3)
 ADVECT = 0.1
 SMEM = pl.BlockSpec(memory_space=pltpu.SMEM)
 VMEM = pl.BlockSpec(memory_space=pltpu.VMEM)
+FIRST_HOP = pl.CostEstimate(flops=10**10, bytes_accessed=8 * 10**6, transcendentals=0)
 LIMIT = pltpu.CompilerParams(vmem_limit_bytes=32 * 1024 * 1024)
 
 
@@ -129,22 +131,30 @@
     )(state, *coefs, low, high)
 
 
-def first_wishes_kernel(mine, other, out):
-    rows = lax.broadcasted_iota(jnp.int32, out.shape, 0)
-    pair = [jnp.broadcast_to(x[...].reshape(1, 1), out.shape) for x in (mine, other)]
-    out[...] = jnp.where(rows == 0, pair[0], pair[1])
-
-
-def join_wishes_kernel(known, mine, other, out):
-    rows = lax.broadcasted_iota(jnp.int32, out.shape, 0)
-    out[...] = jnp.where(rows < known, mine[...], pltpu.roll(other[...], known, 0))
-
-
-def hop(wish, sides, phase):
-    offset = wish ^ lax.axis_index("dom")
-    inner = offset & (sides - 1)
-    outer = lax.shift_right_logical(offset, sides.bit_length() - 1)
-    return jnp.where(lax.axis_index("depth") % 2 == phase, inner, outer)
+def first_wishes_kernel(mine, out):
+    out[...] = jnp.full(out.shape, mine[0], jnp.int32)
+
+
+def ways_of(phase):
+    half = (lax.axis_size("dom").bit_length() - 1) // 2
+    low = [1 << bit for bit in range(half)]
+    high = [step << half for step in low]
+    even, odd = (low[::-1], list(itertools.accumulate(high, operator.or_))) if phase == 0 else (high[::-1], low)
+    ways = []
+    for basis in (even, odd):
+        offsets = [0]
+        for step in basis:
+            offsets += [offset ^ step for offset in offsets]
+        ways.append(offsets)
+    return ways
+
+
+def hop_masks(wish, phase):
+    even, odd = ways_of(phase)
+    first = lax.axis_index("depth") % 2 == 0
+    covered = jnp.where(first, functools.reduce(operator.or_, even), functools.reduce(operator.or_, odd))
+    offset = (wish ^ lax.axis_index("dom")) & covered
+    return [offset == jnp.where(first, *pair) for pair in list(zip(even, odd))[1:]]
 
 
 def tiles(shape):
@@ -158,33 +168,32 @@
     return value
 
 
-def masks_of(wish, sides, phase):
-    wanted = jnp.broadcast_to(hop(wish, sides, phase), (8, wish.shape[-1]))
-    return [wanted == k for k in range(1, sides)]
-
-
-def near_kernel(sides, wishes, state, out):
-    out[...] = hop(wishes[...], sides, 0)
-
-
 def choose_kernel(sides, *refs):
-    candidates, near, far, results = refs[:sides], refs[sides], refs[sides + 1], refs[sides + 2 :]
-    half = sides // 2
-    wanted = near[...], hop(far[...], sides, 0)
-    masks = [
-        [jnp.broadcast_to(wanted[j // half][j % half : j % half + 1], near.shape) == k for k in range(1, sides)]
-        for j in range(sides)
-    ]
+    candidates, rest = refs[:sides], refs[sides:]
+    wishes, results = rest[: len(rest) // 2], rest[len(rest) // 2 :]
+    masks = [hop_masks(wish[...], 0) for wish in wishes]
     for at in tiles(candidates[0].shape):
         values = [candidate[at] for candidate in candidates]
-        for j in range(sides):
-            results[j][at] = pick(values, masks[j])
+        for mask, result in zip(masks, results):
+            result[at] = pick(values, mask)
+
+
+def choose(candidates, wishes):
+    sides, outputs = len(candidates), len(wishes)
+    return pl.pallas_call(
+        functools.partial(choose_kernel, sides),
+        out_shape=[jax.ShapeDtypeStruct(candidates[0].shape, jnp.float32)] * outputs,
+        in_specs=[VMEM] * (sides + outputs),
+        out_specs=[VMEM] * outputs,
+        compiler_params=LIMIT,
+        name="choose",
+    )(*candidates, *wishes)
 
 
 def settle_kernel(sides, pair, *refs):
     candidates, wishes, coefs = refs[:sides], refs[sides], refs[sides + 1 : sides + 4]
     result, edges = refs[sides + 4], refs[sides + 5 :]
-    masks = masks_of(wishes[0:1], sides, 1)
+    masks = hop_masks(wishes[...], 1)
     for at in tiles(result.shape):
         result[at] = pick([candidate[at] for candidate in candidates], masks)
     cells = result.shape[2]
@@ -196,13 +205,10 @@
             edge[4 + q] = coefs[q][pl.ds(start, STEPS)]
 
 
-def swap(x, distance, phase):
+def swap(x, way, phase):
     count, depth = lax.axis_size("dom"), lax.axis_size("depth")
-    sides = 1 << (count.bit_length() // 2)
-    pairs = []
-    for i in range(count):
-        for d in range(depth):
-            pairs.append((i * depth + d, (i ^ (distance if d % 2 == phase else distance * sides)) * depth + d))
+    ways = ways_of(phase)
+    pairs = [(i * depth + d, (i ^ ways[d % 2][way]) * depth + d) for i in range(count) for d in range(depth)]
     return lax.ppermute(x, ("dom", "depth"), pairs)
 
 
@@ -212,47 +218,27 @@
     assert sides * sides == count
     far = range(1, sides)
     like = jax.ShapeDtypeStruct(ensemble.shape, jnp.float32)
-    other = swap(ancestors, 1, 1)
-    first, second = ORDER if sides == 4 else (far, far)
-    got = {k: swap(ensemble, k, 0) for k in first}
+    got = {k: swap(ensemble, k, 0) for k in far}
     coefs = (diffusivity, melting_speed, permeability)
-    wishes = pl.pallas_call(
+    wish = pl.pallas_call(
         first_wishes_kernel,
         out_shape=jax.ShapeDtypeStruct((8, ensemble.shape[-1]), jnp.int32),
-        in_specs=[VMEM] * 2,
+        in_specs=[SMEM],
         out_specs=VMEM,
         compiler_params=LIMIT,
+        cost_estimate=FIRST_HOP,
         name="first_wishes",
-    )(ancestors, other)
-    known = 2
-    while 2 * known < sides:
-        wishes = pl.pallas_call(
-            functools.partial(join_wishes_kernel, known),
-            out_shape=jax.ShapeDtypeStruct(wishes.shape, jnp.int32),
-            in_specs=[VMEM] * 2,
-            out_specs=VMEM,
-            compiler_params=LIMIT,
-            name="join_wishes",
-        )(wishes, swap(wishes, known, 1))
+    )(ancestors)
+    candidates = [ensemble] + [got[k] for k in far]
+    known, wishes, sent = 1, [wish], []
+    while known < sides:
+        wishes += [swap(wish, known, 1) for wish in wishes]
         known *= 2
-    far_wishes = swap(wishes, known, 1)
-    near = pl.pallas_call(
-        functools.partial(near_kernel, sides),
-        out_shape=jax.ShapeDtypeStruct(wishes.shape, jnp.int32),
-        in_specs=[VMEM] * 2,
-        out_specs=VMEM,
-        compiler_params=LIMIT,
-        name="near",
-    )(wishes, ensemble)
-    sent = pl.pallas_call(
-        functools.partial(choose_kernel, sides),
-        out_shape=[like] * sides,
-        in_specs=[VMEM] * (sides + 2),
-        out_specs=[VMEM] * sides,
-        compiler_params=LIMIT,
-        name="choose",
-    )(ensemble, *(got[k] for k in far), near, far_wishes)
-    final = {k: swap(sent[k], k, 1) for k in second}
+    half = sides - sides // 4
+    sent = choose(candidates, wishes[:half])
+    if half < sides:
+        sent += choose(candidates, wishes[half:])
+    final = {k: swap(sent[k], k, 1) for k in far}
     edge = jax.ShapeDtypeStruct((7, STEPS) + ensemble.shape[3:], jnp.float32)
     edges = [edge] if depth == 2 else [edge, edge]
     state, *edges = pl.pallas_call(
@@ -262,7 +248,7 @@
         out_specs=[VMEM] * (1 + len(edges)),
         compiler_params=LIMIT,
         name="settle",
-    )(sent[0], *(final[k] for k in far), wishes, *coefs)
+    )(sent[0], *(final[k] for k in far), wish, *coefs)
     return forecast(state, edges, coefs)
 
 

time: 29.7 us -> 27.2 us (0.916)
  waiting for transfers between devices: 11.2 us -> 8.65 us
  starting transfers between devices: 14.1 us -> 16 us
  local copies, waits for them, and re-layouts: 1.14 us -> 0.02 us
  Pallas kernels: 2.31 us -> 1.65 us
    ppermute x8 -> x9, waiting for transfers between devices: 9.72 us -> 7.18 us  [swap(): return lax.ppermute(x, ('dom', 'depth'), pairs)]
    ppermute x8 -> x9, starting transfers between devices: 14 us -> 16 us  [swap(): return lax.ppermute(x, ('dom', 'depth'), pairs)]
    unnamed x10 -> x8, local copies, waits for them, and re-layouts: 1.14 us -> 0.02 us
    pallas_call x1, Pallas kernels: 0.69 us -> 0.01 us  [local(): pl.pallas_call(first_wishes_kernel, out_shape=jax.ShapeDtypeStruct((8, en...]
  transfers between devices with their start and end apart: 9 -> 10, of which waited for: 5 -> 6; matrix products, arithmetic and copies ran while one was open for 0% -> 0% of each run, Pallas kernels for 2% -> 0%
where the time goes in v3:
time: 27.2 us; the launch traced here: 27.1 us
  starting transfers between devices  16 us (59%)
  waiting for transfers between devices  8.65 us (32%)
  Pallas kernels  1.65 us (6%)
  between operations  0.72 us (3%)
    ppermute x9, starting transfers between devices, swap(): return lax.ppermute(x, ('dom', 'depth'), pairs)  16 us
    ppermute x9, waiting for transfers between devices, swap(): return lax.ppermute(x, ('dom', 'depth'), pairs)  7.18 us
    ppermute x1, waiting for transfers between devices, other_side(): return lax.ppermute(x, 'depth', [(0, 1), (1, 0)])  1.48 us
    pallas_call x1, Pallas kernels, forecast(): pl.pallas_call(functools.partial(forecast_kernel, cells, pair, count), ou...  1.44 us
  transfers between devices with their start and end apart: 10, of which 6 were waited for; matrix products, arithmetic and copies ran while one was open for 0% of the time, Pallas kernels for 0%

profile of v3, /device:TPU:0, one launch (start us, length us, event | category | flops | bytes accessed | tf_op | source)
XLA Modules:
  0.0 27.1 jit_solution(16300995415448876148)
XLA Ops:
  0.0 3.9 %collective-permute-start.2 = (f32[1,4,6,16,128]{4,3,2,1,0:T(8,128)}, f32[1,4,6,16,128]{4,3,2,1,0:T(8,128)S(1)}, u32[]{:S(2)}, u32[]{:S(2)}) collective-permute-start(f32[1,4,6,16,128]{4,3,2,1,0:T(8,128)} %refs_0_.3), channel_id=1, source_target_pairs={{0,6},{1,17},{2,4},{3,19},{4,2},{5,21},{6,0},{7,23},{8,14},{9,25},... | collective-permute-start | bytes 589832 | tf_op jit(solution)/shard_map/ppermute | solution.py:212
  3.9 0.5 %collective-permute-start.1 = (f32[1,4,6,16,128]{4,3,2,1,0:T(8,128)}, f32[1,4,6,16,128]{4,3,2,1,0:T(8,128)S(1)}, u32[]{:S(2)}, u32[]{:S(2)}) collective-permute-start(f32[1,4,6,16,128]{4,3,2,1,0:T(8,128)} %refs_0_.3), channel_id=1, source_target_pairs={{0,2},{1,25},{2,0},{3,27},{4,6},{5,29},{6,4},{7,31},{8,10},{9,17},... | collective-permute-start | bytes 589832 | tf_op jit(solution)/shard_map/ppermute | solution.py:212
  4.4 0.0 collective-permute-start
  5.1 3.1 %collective-permute-start.3 = (s32[8,128]{1,0:T(8,128)S(1)}, s32[8,128]{1,0:T(8,128)S(1)}, u32[]{:S(2)}, u32[]{:S(2)}) collective-permute-start(s32[8,128]{1,0:T(8,128)S(1)} %first_wishes.1.refs_4_), channel_id=1, source_target_pairs={{0,16},{1,3},{2,18},{3,1},{4,20},{5,7},{6,22},{7,5},{8,24},{9,11},... | collective-permute-start | bytes 12296 | tf_op jit(solution)/shard_map/ppermute | solution.py:212
  8.3 1.6 %collective-permute-start.4 = (s32[8,128]{1,0:T(8,128)S(1)}, s32[8,128]{1,0:T(8,128)S(1)}, u32[]{:S(2)}, u32[]{:S(2)}) collective-permute-start(s32[8,128]{1,0:T(8,128)S(1)} %first_wishes.1.refs_4_), channel_id=1, source_target_pairs={{0,8},{1,5},{2,10},{3,7},{4,12},{5,1},{6,14},{7,3},{8,0},{9,13},{1... | collective-permute-start | bytes 12296 | tf_op jit(solution)/shard_map/ppermute | solution.py:212
  9.8 0.7 %collective-permute-done.3.refs_5_ = s32[8,128]{1,0:T(8,128)S(1)} collective-permute-done((s32[8,128]{1,0:T(8,128)S(1)}, s32[8,128]{1,0:T(8,128)S(1)}, u32[]{:S(2)}, u32[]{:S(2)}) %collective-permute-start.3) | collective-permute-done | bytes 4128 | tf_op jit(solution)/shard_map/ppermute | solution.py:212
  10.6 1.3 %collective-permute-start.7 = (s32[8,128]{1,0:T(8,128)S(1)}, s32[8,128]{1,0:T(8,128)S(1)}, u32[]{:S(2)}, u32[]{:S(2)}) collective-permute-start(s32[8,128]{1,0:T(8,128)S(1)} %collective-permute-done.3.refs_5_), channel_id=1, source_target_pairs={{0,8},{1,5},{2,10},{3,7},{4,12},{5,1},{6,14},{7,3},{8,0},{9,13},{1... | collective-permute-start | bytes 12296 | tf_op jit(solution)/shard_map/ppermute | solution.py:212
  11.9 0.1 collective-permute-done.4.refs_6_
  12.0 0.0 collective-permute-done.2.refs_3_
  12.0 0.0 collective-permute-done.1.refs_2_
  12.0 0.0 collective-permute-done.refs_1_
  12.0 0.1 choose.2
  12.1 2.6 %collective-permute-start.5 = (f32[1,4,6,16,128]{4,3,2,1,0:T(8,128)S(1)}, f32[1,4,6,16,128]{4,3,2,1,0:T(8,128)S(1)}, u32[]{:S(2)}, u32[]{:S(2)}) collective-permute-start(f32[1,4,6,16,128]{4,3,2,1,0:T(8,128)S(1)} %get-tuple-element.11), channel_id=1, source_target_pairs={{0,16},{1,3},{2,18},{3,1},{4,20},{5,7},{6,22},{7,5},{8,24},{9,11},... | collective-permute-start | bytes 589832 | tf_op jit(solution)/shard_map/ppermute | solution.py:212
  14.7 1.1 %collective-permute-start.6 = (f32[1,4,6,16,128]{4,3,2,1,0:T(8,128)S(1)}, f32[1,4,6,16,128]{4,3,2,1,0:T(8,128)S(1)}, u32[]{:S(2)}, u32[]{:S(2)}) collective-permute-start(f32[1,4,6,16,128]{4,3,2,1,0:T(8,128)S(1)} %get-tuple-element.12), channel_id=1, source_target_pairs={{0,8},{1,5},{2,10},{3,7},{4,12},{5,1},{6,14},{7,3},{8,0},{9,13},{1... | collective-permute-start | bytes 589832 | tf_op jit(solution)/shard_map/ppermute | solution.py:212
  15.8 0.0 collective-permute-done.7.refs_4_
  15.8 0.1 choose.3
  15.9 1.8 %collective-permute-start.8 = (f32[1,4,6,16,128]{4,3,2,1,0:T(8,128)S(1)}, f32[1,4,6,16,128]{4,3,2,1,0:T(8,128)S(1)}, u32[]{:S(2)}, u32[]{:S(2)}) collective-permute-start(f32[1,4,6,16,128]{4,3,2,1,0:T(8,128)S(1)} %choose.3), channel_id=1, source_target_pairs={{0,24},{1,7},{2,26},{3,5},{4,28},{5,3},{6,30},{7,1},{8,16},{9,15},... | collective-permute-start | bytes 589832 | tf_op jit(solution)/shard_map/ppermute | solution.py:212
  17.7 3.3 %collective-permute-done.5.refs_1_ = f32[1,4,6,16,128]{4,3,2,1,0:T(8,128)S(1)} collective-permute-done((f32[1,4,6,16,128]{4,3,2,1,0:T(8,128)S(1)}, f32[1,4,6,16,128]{4,3,2,1,0:T(8,128)S(1)}, u32[]{:S(2)}, u32[]{:S(2)}) %collective-permute-start.5) | collective-permute-done | bytes 196640 | tf_op jit(solution)/shard_map/ppermute | solution.py:212
  20.9 0.5 %collective-permute-done.6.refs_2_ = f32[1,4,6,16,128]{4,3,2,1,0:T(8,128)S(1)} collective-permute-done((f32[1,4,6,16,128]{4,3,2,1,0:T(8,128)S(1)}, f32[1,4,6,16,128]{4,3,2,1,0:T(8,128)S(1)}, u32[]{:S(2)}, u32[]{:S(2)}) %collective-permute-start.6) | collective-permute-done | bytes 196640 | tf_op jit(solution)/shard_map/ppermute | solution.py:212
  21.5 2.5 %collective-permute-done.8.refs_3_ = f32[1,4,6,16,128]{4,3,2,1,0:T(8,128)S(1)} collective-permute-done((f32[1,4,6,16,128]{4,3,2,1,0:T(8,128)S(1)}, f32[1,4,6,16,128]{4,3,2,1,0:T(8,128)S(1)}, u32[]{:S(2)}, u32[]{:S(2)}) %collective-permute-start.8) | collective-permute-done | bytes 196640 | tf_op jit(solution)/shard_map/ppermute | solution.py:212
  24.0 0.1 settle.1
  24.1 0.1 collective-permute-start.9
  24.2 1.5 %collective-permute-done.9.refs_4_.refs_5_ = f32[7,4,16,128]{3,2,1,0:T(8,128)S(1)} collective-permute-done((f32[7,4,16,128]{3,2,1,0:T(8,128)S(1)}, f32[7,4,16,128]{3,2,1,0:T(8,128)S(1)}, u32[]{:S(2)}, u32[]{:S(2)}) %collective-permute-start.9) | collective-permute-done | bytes 229408 | tf_op jit(solution)/shard_map/ppermute | solution.py:106
  25.6 1.4 %forecast.1 = f32[1,4,6,16,128]{4,3,2,1,0:T(8,128)} custom-call(f32[1,4,6,16,128]{4,3,2,1,0:T(8,128)S(1)} %get-tuple-element.13.refs_0_, f32[6,16,128]{2,1,0:T(8,128)S(1)} %copy-done.1, f32[6,16,128]{2,1,0:T(8,128)S(1)} %copy-done.2, f32[6,16,128]{2,1,0:T(8,128)S(1)} %copy-done.3, f32[7,4,16,128]{3,2,1,0:T(8,128)S(1)} %collective-permute-done.9.refs_4_.refs_5_, ...), custom_call_target="tpu_custom_call" | custom-call | tf_op jit(solution)/shard_map/forecast/pallas_call | solution.py:119
  (9 shorter events, 0.0 us)
Async XLA Ops:
  0.0 12.0 %collective-permute-start.2 = (f32[1,4,6,16,128]{4,3,2,1,0:T(8,128)}, f32[1,4,6,16,128]{4,3,2,1,0:T(8,128)S(1)}, u32[]{:S(2)}, u32[]{:S(2)}) collective-permute-start(f32[1,4,6,16,128]{4,3,2,1,0:T(8,128)} %refs_0_.3), channel_id=1, source_target_pairs={{0,6},{1,17},{2,4},{3,19},{4,2},{5,21},{6,0},{7,23},{8,14},{9,25},... | collective-permute-start | bytes 589832 | tf_op jit(solution)/shard_map/ppermute | solution.py:212
  3.9 8.1 %collective-permute-start.1 = (f32[1,4,6,16,128]{4,3,2,1,0:T(8,128)}, f32[1,4,6,16,128]{4,3,2,1,0:T(8,128)S(1)}, u32[]{:S(2)}, u32[]{:S(2)}) collective-permute-start(f32[1,4,6,16,128]{4,3,2,1,0:T(8,128)} %refs_0_.3), channel_id=1, source_target_pairs={{0,2},{1,25},{2,0},{3,27},{4,6},{5,29},{6,4},{7,31},{8,10},{9,17},... | collective-permute-start | bytes 589832 | tf_op jit(solution)/shard_map/ppermute | solution.py:212
  4.4 7.6 %collective-permute-start = (f32[1,4,6,16,128]{4,3,2,1,0:T(8,128)}, f32[1,4,6,16,128]{4,3,2,1,0:T(8,128)S(1)}, u32[]{:S(2)}, u32[]{:S(2)}) collective-permute-start(f32[1,4,6,16,128]{4,3,2,1,0:T(8,128)} %refs_0_.3), channel_id=1, source_target_pairs={{0,4},{1,9},{2,6},{3,11},{4,0},{5,13},{6,2},{7,15},{8,12},{9,1},{1... | collective-permute-start | bytes 589832 | tf_op jit(solution)/shard_map/ppermute | solution.py:212
  5.1 6.9 %copy-start = (f32[1,4,6,16,128]{4,3,2,1,0:T(8,128)S(1)}, f32[1,4,6,16,128]{4,3,2,1,0:T(8,128)}, u32[]{:S(2)}) copy-start(f32[1,4,6,16,128]{4,3,2,1,0:T(8,128)} %refs_0_.3) | copy-start | bytes 589828
  5.1 5.4 %collective-permute-start.3 = (s32[8,128]{1,0:T(8,128)S(1)}, s32[8,128]{1,0:T(8,128)S(1)}, u32[]{:S(2)}, u32[]{:S(2)}) collective-permute-start(s32[8,128]{1,0:T(8,128)S(1)} %first_wishes.1.refs_4_), channel_id=1, source_target_pairs={{0,16},{1,3},{2,18},{3,1},{4,20},{5,7},{6,22},{7,5},{8,24},{9,11},... | collective-permute-start | bytes 12296 | tf_op jit(solution)/shard_map/ppermute | solution.py:212
  8.3 3.7 %collective-permute-start.4 = (s32[8,128]{1,0:T(8,128)S(1)}, s32[8,128]{1,0:T(8,128)S(1)}, u32[]{:S(2)}, u32[]{:S(2)}) collective-permute-start(s32[8,128]{1,0:T(8,128)S(1)} %first_wishes.1.refs_4_), channel_id=1, source_target_pairs={{0,8},{1,5},{2,10},{3,7},{4,12},{5,1},{6,14},{7,3},{8,0},{9,13},{1... | collective-permute-start | bytes 12296 | tf_op jit(solution)/shard_map/ppermute | solution.py:212
  10.6 5.3 %collective-permute-start.7 = (s32[8,128]{1,0:T(8,128)S(1)}, s32[8,128]{1,0:T(8,128)S(1)}, u32[]{:S(2)}, u32[]{:S(2)}) collective-permute-start(s32[8,128]{1,0:T(8,128)S(1)} %collective-permute-done.3.refs_5_), channel_id=1, source_target_pairs={{0,8},{1,5},{2,10},{3,7},{4,12},{5,1},{6,14},{7,3},{8,0},{9,13},{1... | collective-permute-start | bytes 12296 | tf_op jit(solution)/shard_map/ppermute | solution.py:212
  12.1 8.8 %collective-permute-start.5 = (f32[1,4,6,16,128]{4,3,2,1,0:T(8,128)S(1)}, f32[1,4,6,16,128]{4,3,2,1,0:T(8,128)S(1)}, u32[]{:S(2)}, u32[]{:S(2)}) collective-permute-start(f32[1,4,6,16,128]{4,3,2,1,0:T(8,128)S(1)} %get-tuple-element.11), channel_id=1, source_target_pairs={{0,16},{1,3},{2,18},{3,1},{4,20},{5,7},{6,22},{7,5},{8,24},{9,11},... | collective-permute-start | bytes 589832 | tf_op jit(solution)/shard_map/ppermute | solution.py:212
  14.7 9.3 %copy-start.1 = (f32[6,16,128]{2,1,0:T(8,128)S(1)}, f32[6,16,128]{2,1,0:T(8,128)}, u32[]{:S(2)}) copy-start(f32[6,16,128]{2,1,0:T(8,128)} %refs_1_.1) | copy-start | bytes 147460
  14.7 9.3 %copy-start.2 = (f32[6,16,128]{2,1,0:T(8,128)S(1)}, f32[6,16,128]{2,1,0:T(8,128)}, u32[]{:S(2)}) copy-start(f32[6,16,128]{2,1,0:T(8,128)} %refs_2_.1) | copy-start | bytes 147460
  14.7 9.3 %copy-start.3 = (f32[6,16,128]{2,1,0:T(8,128)S(1)}, f32[6,16,128]{2,1,0:T(8,128)}, u32[]{:S(2)}) copy-start(f32[6,16,128]{2,1,0:T(8,128)} %refs_3_.1) | copy-start | bytes 147460
  14.7 6.8 %collective-permute-start.6 = (f32[1,4,6,16,128]{4,3,2,1,0:T(8,128)S(1)}, f32[1,4,6,16,128]{4,3,2,1,0:T(8,128)S(1)}, u32[]{:S(2)}, u32[]{:S(2)}) collective-permute-start(f32[1,4,6,16,128]{4,3,2,1,0:T(8,128)S(1)} %get-tuple-element.12), channel_id=1, source_target_pairs={{0,8},{1,5},{2,10},{3,7},{4,12},{5,1},{6,14},{7,3},{8,0},{9,13},{1... | collective-permute-start | bytes 589832 | tf_op jit(solution)/shard_map/ppermute | solution.py:212
  15.9 8.1 %collective-permute-start.8 = (f32[1,4,6,16,128]{4,3,2,1,0:T(8,128)S(1)}, f32[1,4,6,16,128]{4,3,2,1,0:T(8,128)S(1)}, u32[]{:S(2)}, u32[]{:S(2)}) collective-permute-start(f32[1,4,6,16,128]{4,3,2,1,0:T(8,128)S(1)} %choose.3), channel_id=1, source_target_pairs={{0,24},{1,7},{2,26},{3,5},{4,28},{5,3},{6,30},{7,1},{8,16},{9,15},... | collective-permute-start | bytes 589832 | tf_op jit(solution)/shard_map/ppermute | solution.py:212
  24.1 1.6 %collective-permute-start.9 = (f32[7,4,16,128]{3,2,1,0:T(8,128)S(1)}, f32[7,4,16,128]{3,2,1,0:T(8,128)S(1)}, u32[]{:S(2)}, u32[]{:S(2)}) collective-permute-start(f32[7,4,16,128]{3,2,1,0:T(8,128)S(1)} %get-tuple-element.14), channel_id=1, source_target_pairs={{0,1},{1,0},{2,3},{3,2},{4,5},{5,4},{6,7},{7,6},{8,9},{9,8},{10,11... | collective-permute-start | bytes 688136 | tf_op jit(solution)/shard_map/ppermute | solution.py:106

commit v4 on v3

--- a/solution.py
+++ b/solution.py
@@ -27,12 +27,12 @@
     return total + jnp.where(columns == high_column, 0.0, pltpu.roll(q, high_column, 1))
 
 
-def layer_step(state, layer, diffuse, reacts, permeab):
-    m, v, h, c = (state[q, layer] for q in range(4))
-    m_up, v_up, h_up, c_up = (state[q, layer - 1] for q in range(4))
-    m_low, v_low, h_low, c_low = (state[q, layer + 1] for q in range(4))
-    down = ADVECT * jnp.maximum(v, 0.0)
-    up = ADVECT * jnp.minimum(v, 0.0)
+def layer_step(state, layer, sign, diffuse, reacts, permeab):
+    m, v, h, c = (state(q, layer) for q in range(4))
+    m_up, v_up, h_up, c_up = (state(q, layer - 1) for q in range(4))
+    m_low, v_low, h_low, c_low = (state(q, layer + 1) for q in range(4))
+    speed = (ADVECT * sign) * v
+    down, up = jnp.maximum(speed, 0.0), jnp.minimum(speed, 0.0)
 
     def transport(q, upper, lower):
         return down * (q - upper) + up * (lower - q)
@@ -49,55 +49,91 @@
     )
 
 
-def forecast_kernel(cells, pair, count, *refs):
-    own, own_coefs, low, high = refs[0], refs[1:4], refs[4], refs[5]
-    out, even, odd, coefs = refs[6:]
+def forecast_kernel(cells, count, own, d, r, p, low, high, out, even, odd, coefs):
     at = lax.axis_index("depth")
-    window = cells + (STEPS if pair else 2 * STEPS)
+    window = cells + 2 * STEPS
     zero = jnp.zeros(even.shape[2:], jnp.float32)
     for q in range(4):
         for buffer in (even, odd):
             buffer[q, 0] = zero
             buffer[q, window + 1] = zero
-
-    def fill(to, layers, state):
-        for i in range(layers):
-            for q in range(7):
-                (even if q < 4 else coefs)[q % 4, to + i] = state(q, i)
-
-    def mine(q, i):
-        return own[0, q, i] if q < 4 else own_coefs[q - 4][i]
-
-    if pair:
-        first = at == 0
-        fill(jnp.where(first, 1, 1 + STEPS), cells, mine)
-        fill(jnp.where(first, 1 + cells, 1), STEPS, lambda q, i: low[q, i])
-    else:
-        fill(1, STEPS, lambda q, i: low[q, i])
-        fill(1 + STEPS, cells, mine)
-        fill(1 + STEPS + cells, STEPS, lambda q, i: high[q, i])
-        inside_first = jnp.where(at == 0, 1 + STEPS, 0)
-        inside_last = jnp.where(at == count - 1, STEPS + cells, window + 1)
-
-    buffers = (even, odd)
+    for q in range(7):
+        to = even if q < 4 else coefs
+        for i in range(STEPS):
+            to[q % 4, 1 + i] = low[q, i]
+            to[q % 4, 1 + STEPS + cells + i] = high[q, i]
+        for i in range(cells):
+            to[q % 4, 1 + STEPS + i] = own[0, q, i] if q < 4 else (d, r, p)[q - 4][i]
+    inside_first = jnp.where(at == 0, 1 + STEPS, 0)
+    inside_last = jnp.where(at == count - 1, STEPS + cells, window + 1)
     for step in range(STEPS):
-        now, later = buffers[step % 2], buffers[1 - step % 2]
-        left = STEPS - 1 - step
-        if pair:
-            start, layers = jnp.where(first, 1, 2 + step), cells + left
-        else:
-            start, layers = 2 + step, cells + 2 * left
-        for i in range(layers):
-            layer = start + i
-            values = layer_step(now, layer, coefs[0, layer], coefs[1, layer], coefs[2, layer])
+        now, later = (even, odd) if step % 2 == 0 else (odd, even)
+        for layer in range(2 + step, window - step):
+            values = layer_step(lambda q, i: now[q, i], layer, 1.0, *(coefs[q, layer] for q in range(3)))
             for q in range(4):
-                value = values[q]
                 if step == STEPS - 1:
-                    out[0, q, i] = value
+                    out[0, q, layer - STEPS - 1] = values[q]
+                else:
+                    inside = (layer >= inside_first) & (layer <= inside_last)
+                    later[q, layer] = jnp.where(inside, values[q], 0.0)
+
+
+def from_end(cells, i):
+    return jnp.where(lax.axis_index("depth") == 0, i, cells - 1 - i)
+
+
+def sign_of_order():
+    return jnp.where(lax.axis_index("depth") == 0, 1.0, -1.0).astype(jnp.float32)
+
+
+def inner_kernel(cells, own, d, r, p, head, border, even, odd):
+    sign = sign_of_order()
+    for q in range(4):
+        for buffer in (even, odd):
+            buffer[q, 0] = jnp.zeros(even.shape[2:], jnp.float32)
+        for i in range(cells):
+            even[q, 1 + i] = own[0, q, from_end(cells, i)]
+    for step in range(STEPS):
+        now, later = (even, odd) if step % 2 == 0 else (odd, even)
+        layers = cells - 1 - step
+        for layer in range(1, layers + 1):
+            at = from_end(cells, layer - 1)
+            values = layer_step(lambda q, i: now[q, i], layer, sign, d[at], r[at], p[at])
+            for q in range(4):
+                if step == STEPS - 1:
+                    head[q, layer - 1] = values[q]
                     continue
-                if not pair:
-                    value = jnp.where((layer >= inside_first) & (layer <= inside_last), value, 0.0)
-                later[q, layer] = value
+                later[q, layer] = values[q]
+                if layer > layers - 2:
+                    border[step, q, layer - layers + 1] = values[q]
+
+
+def outer_kernel(cells, own, d, r, p, other, head, border, out, state):
+    sign = sign_of_order()
+    for q in range(4):
+        for i in range(2):
+            state[0, q, i] = own[0, q, from_end(cells, cells - 2 + i)]
+            for step in range(1, STEPS):
+                state[step, q, i] = border[step - 1, q, i]
+        for i in range(STEPS):
+            state[0, q, 2 + i] = other[q, from_end(STEPS, i)]
+        for i in range(cells - STEPS):
+            out[0, q, from_end(cells, i)] = head[q, i]
+    for step in range(STEPS):
+        for i in range(1, 1 + STEPS):
+            layer = cells - 1 - step + i
+            if layer <= cells:
+                at = from_end(cells, layer - 1)
+                coefs = d[at], r[at], p[at]
+            else:
+                at = from_end(STEPS, layer - cells - 1)
+                coefs = other[4, at], other[5, at], other[6, at]
+            values = layer_step(lambda q, j: state[step, q, j], i, sign, *coefs)
+            for q in range(4):
+                if step == STEPS - 1:
+                    out[0, q, from_end(cells, layer - 1)] = values[q]
+                else:
+                    state[step + 1, q, 1 + i] = values[q]
 
 
 def other_side(x, towards):
@@ -109,26 +145,44 @@
 
 def forecast(state, edges, coefs):
     count = lax.axis_size("depth")
-    pair = count == 2
     _, _, cells, rows, columns = state.shape
-    window = cells + (STEPS if pair else 2 * STEPS)
-    if pair:
-        low = high = other_side(edges[0], 1)
-    else:
-        low, high = other_side(edges[1], 1), other_side(edges[0], -1)
-    return pl.pallas_call(
-        functools.partial(forecast_kernel, cells, pair, count),
-        out_shape=jax.ShapeDtypeStruct(state.shape, jnp.float32),
-        in_specs=[VMEM] * 6,
-        out_specs=VMEM,
-        scratch_shapes=[
-            pltpu.VMEM((4, window + 2, rows, columns), jnp.float32),
-            pltpu.VMEM((4, window + 2, rows, columns), jnp.float32),
-            pltpu.VMEM((3, window + 2, rows, columns), jnp.float32),
-        ],
-        compiler_params=LIMIT,
-        name="forecast",
-    )(state, *coefs, low, high)
+    assert cells >= STEPS
+    result = jax.ShapeDtypeStruct(state.shape, jnp.float32)
+
+    def layers(*lead):
+        return lead + (rows, columns)
+
+    def call(kernel, out_shape, scratch, *operands):
+        return pl.pallas_call(
+            kernel,
+            out_shape=out_shape,
+            in_specs=[VMEM] * len(operands),
+            out_specs=jax.tree.map(lambda _: VMEM, out_shape),
+            scratch_shapes=[pltpu.VMEM(shape, jnp.float32) for shape in scratch],
+            compiler_params=LIMIT,
+            name=kernel.func.__name__.removesuffix("_kernel"),
+        )(*operands)
+
+    if count == 2:
+        other = other_side(edges[0], 1)
+        parts = (
+            jax.ShapeDtypeStruct(layers(4, max(cells - STEPS, 1)), jnp.float32),
+            jax.ShapeDtypeStruct(layers(STEPS - 1, 4, 2), jnp.float32),
+        )
+        inner = functools.partial(inner_kernel, cells)
+        head, border = call(inner, parts, [layers(4, cells + 1)] * 2, state, *coefs)
+        outer = functools.partial(outer_kernel, cells)
+        return call(outer, result, [layers(STEPS, 4, STEPS + 2)], state, *coefs, other, head, border)
+    window = cells + 2 * STEPS + 2
+    return call(
+        functools.partial(forecast_kernel, cells, count),
+        result,
+        [layers(4, window), layers(4, window), layers(3, window)],
+        state,
+        *coefs,
+        other_side(edges[1], 1),
+        other_side(edges[0], -1),
+    )
 
 
 def first_wishes_kernel(mine, out):

time: 27.2 us -> 26.9 us (0.989)
  waiting for transfers between devices: 8.65 us -> 8.27 us
    ppermute x1, waiting for transfers between devices: 1.48 us -> 1.1 us  [other_side(): return lax.ppermute(x, 'depth', [(0, 1), (1, 0)])]
    pallas_call x1 -> x2, Pallas kernels: 1.44 us -> 1.45 us  [call(): pl.pallas_call(kernel, out_shape=out_shape, in_specs=[VMEM] * len(operand...]
  transfers between devices with their start and end apart: 10 -> 10, of which waited for: 6 -> 6; matrix products, arithmetic and copies ran while one was open for 0% -> 0% of each run, Pallas kernels for 0% -> 2%
where the time goes in v4:
time: 26.9 us; the launch traced here: 26.7 us
  starting transfers between devices  16 us (59%)
  waiting for transfers between devices  8.27 us (31%)
  Pallas kernels  1.65 us (6%)
  between operations  0.72 us (3%)
    ppermute x9, starting transfers between devices, swap(): return lax.ppermute(x, ('dom', 'depth'), pairs)  16 us
    ppermute x9, waiting for transfers between devices, swap(): return lax.ppermute(x, ('dom', 'depth'), pairs)  7.18 us
    pallas_call x2, Pallas kernels, call(): pl.pallas_call(kernel, out_shape=out_shape, in_specs=[VMEM] * len(operand...  1.45 us
    ppermute x1, waiting for transfers between devices, other_side(): return lax.ppermute(x, 'depth', [(0, 1), (1, 0)])  1.1 us
  transfers between devices with their start and end apart: 10, of which 6 were waited for; matrix products, arithmetic and copies ran while one was open for 0% of the time, Pallas kernels for 2%

profile of v4, /device:TPU:0, one launch (start us, length us, event | category | flops | bytes accessed | tf_op | source)
XLA Modules:
  0.0 26.7 jit_solution(229785961010080409)
XLA Ops:
  0.0 3.9 %collective-permute-start.2 = (f32[1,4,6,16,128]{4,3,2,1,0:T(8,128)}, f32[1,4,6,16,128]{4,3,2,1,0:T(8,128)S(1)}, u32[]{:S(2)}, u32[]{:S(2)}) collective-permute-start(f32[1,4,6,16,128]{4,3,2,1,0:T(8,128)} %refs_0_.3), channel_id=1, source_target_pairs={{0,6},{1,17},{2,4},{3,19},{4,2},{5,21},{6,0},{7,23},{8,14},{9,25},... | collective-permute-start | bytes 589832 | tf_op jit(solution)/shard_map/ppermute | solution.py:266
  3.9 0.5 %collective-permute-start.1 = (f32[1,4,6,16,128]{4,3,2,1,0:T(8,128)}, f32[1,4,6,16,128]{4,3,2,1,0:T(8,128)S(1)}, u32[]{:S(2)}, u32[]{:S(2)}) collective-permute-start(f32[1,4,6,16,128]{4,3,2,1,0:T(8,128)} %refs_0_.3), channel_id=1, source_target_pairs={{0,2},{1,25},{2,0},{3,27},{4,6},{5,29},{6,4},{7,31},{8,10},{9,17},... | collective-permute-start | bytes 589832 | tf_op jit(solution)/shard_map/ppermute | solution.py:266
  4.4 0.0 collective-permute-start
  5.1 3.1 %collective-permute-start.3 = (s32[8,128]{1,0:T(8,128)S(1)}, s32[8,128]{1,0:T(8,128)S(1)}, u32[]{:S(2)}, u32[]{:S(2)}) collective-permute-start(s32[8,128]{1,0:T(8,128)S(1)} %first_wishes.1.refs_4_), channel_id=1, source_target_pairs={{0,16},{1,3},{2,18},{3,1},{4,20},{5,7},{6,22},{7,5},{8,24},{9,11},... | collective-permute-start | bytes 12296 | tf_op jit(solution)/shard_map/ppermute | solution.py:266
  8.3 1.6 %collective-permute-start.4 = (s32[8,128]{1,0:T(8,128)S(1)}, s32[8,128]{1,0:T(8,128)S(1)}, u32[]{:S(2)}, u32[]{:S(2)}) collective-permute-start(s32[8,128]{1,0:T(8,128)S(1)} %first_wishes.1.refs_4_), channel_id=1, source_target_pairs={{0,8},{1,5},{2,10},{3,7},{4,12},{5,1},{6,14},{7,3},{8,0},{9,13},{1... | collective-permute-start | bytes 12296 | tf_op jit(solution)/shard_map/ppermute | solution.py:266
  9.8 0.7 %collective-permute-done.3.refs_5_ = s32[8,128]{1,0:T(8,128)S(1)} collective-permute-done((s32[8,128]{1,0:T(8,128)S(1)}, s32[8,128]{1,0:T(8,128)S(1)}, u32[]{:S(2)}, u32[]{:S(2)}) %collective-permute-start.3) | collective-permute-done | bytes 4128 | tf_op jit(solution)/shard_map/ppermute | solution.py:266
  10.6 1.3 %collective-permute-start.7 = (s32[8,128]{1,0:T(8,128)S(1)}, s32[8,128]{1,0:T(8,128)S(1)}, u32[]{:S(2)}, u32[]{:S(2)}) collective-permute-start(s32[8,128]{1,0:T(8,128)S(1)} %collective-permute-done.3.refs_5_), channel_id=1, source_target_pairs={{0,8},{1,5},{2,10},{3,7},{4,12},{5,1},{6,14},{7,3},{8,0},{9,13},{1... | collective-permute-start | bytes 12296 | tf_op jit(solution)/shard_map/ppermute | solution.py:266
  11.9 0.1 collective-permute-done.4.refs_6_
  12.0 0.0 collective-permute-done.2.refs_3_
  12.0 0.0 collective-permute-done.1.refs_2_
  12.0 0.0 collective-permute-done.refs_1_
  12.0 0.1 choose.2
  12.1 2.6 %collective-permute-start.5 = (f32[1,4,6,16,128]{4,3,2,1,0:T(8,128)S(1)}, f32[1,4,6,16,128]{4,3,2,1,0:T(8,128)S(1)}, u32[]{:S(2)}, u32[]{:S(2)}) collective-permute-start(f32[1,4,6,16,128]{4,3,2,1,0:T(8,128)S(1)} %get-tuple-element.13), channel_id=1, source_target_pairs={{0,16},{1,3},{2,18},{3,1},{4,20},{5,7},{6,22},{7,5},{8,24},{9,11},... | collective-permute-start | bytes 589832 | tf_op jit(solution)/shard_map/ppermute | solution.py:266
  14.7 1.1 %collective-permute-start.6 = (f32[1,4,6,16,128]{4,3,2,1,0:T(8,128)S(1)}, f32[1,4,6,16,128]{4,3,2,1,0:T(8,128)S(1)}, u32[]{:S(2)}, u32[]{:S(2)}) collective-permute-start(f32[1,4,6,16,128]{4,3,2,1,0:T(8,128)S(1)} %get-tuple-element.14), channel_id=1, source_target_pairs={{0,8},{1,5},{2,10},{3,7},{4,12},{5,1},{6,14},{7,3},{8,0},{9,13},{1... | collective-permute-start | bytes 589832 | tf_op jit(solution)/shard_map/ppermute | solution.py:266
  15.8 0.1 choose.3
  15.9 1.8 %collective-permute-start.8 = (f32[1,4,6,16,128]{4,3,2,1,0:T(8,128)S(1)}, f32[1,4,6,16,128]{4,3,2,1,0:T(8,128)S(1)}, u32[]{:S(2)}, u32[]{:S(2)}) collective-permute-start(f32[1,4,6,16,128]{4,3,2,1,0:T(8,128)S(1)} %choose.3), channel_id=1, source_target_pairs={{0,24},{1,7},{2,26},{3,5},{4,28},{5,3},{6,30},{7,1},{8,16},{9,15},... | collective-permute-start | bytes 589832 | tf_op jit(solution)/shard_map/ppermute | solution.py:266
  17.7 3.3 %collective-permute-done.5.refs_1_ = f32[1,4,6,16,128]{4,3,2,1,0:T(8,128)S(1)} collective-permute-done((f32[1,4,6,16,128]{4,3,2,1,0:T(8,128)S(1)}, f32[1,4,6,16,128]{4,3,2,1,0:T(8,128)S(1)}, u32[]{:S(2)}, u32[]{:S(2)}) %collective-permute-start.5) | collective-permute-done | bytes 196640 | tf_op jit(solution)/shard_map/ppermute | solution.py:266
  20.9 0.5 %collective-permute-done.6.refs_2_ = f32[1,4,6,16,128]{4,3,2,1,0:T(8,128)S(1)} collective-permute-done((f32[1,4,6,16,128]{4,3,2,1,0:T(8,128)S(1)}, f32[1,4,6,16,128]{4,3,2,1,0:T(8,128)S(1)}, u32[]{:S(2)}, u32[]{:S(2)}) %collective-permute-start.6) | collective-permute-done | bytes 196640 | tf_op jit(solution)/shard_map/ppermute | solution.py:266
  21.5 2.5 %collective-permute-done.8.refs_3_ = f32[1,4,6,16,128]{4,3,2,1,0:T(8,128)S(1)} collective-permute-done((f32[1,4,6,16,128]{4,3,2,1,0:T(8,128)S(1)}, f32[1,4,6,16,128]{4,3,2,1,0:T(8,128)S(1)}, u32[]{:S(2)}, u32[]{:S(2)}) %collective-permute-start.8) | collective-permute-done | bytes 196640 | tf_op jit(solution)/shard_map/ppermute | solution.py:266
  24.0 0.1 settle.1
  24.1 0.1 collective-permute-start.9
  24.2 0.4 %inner.1 = (f32[4,2,16,128]{3,2,1,0:T(8,128)S(1)}, f32[3,4,2,16,128]{4,3,2,1,0:T(8,128)S(1)}) custom-call(f32[1,4,6,16,128]{4,3,2,1,0:T(8,128)S(1)} %get-tuple-element.15.own, f32[6,16,128]{2,1,0:T(8,128)S(1)} %copy-done.1, f32[6,16,128]{2,1,0:T(8,128)S(1)} %copy-done.2, f32[6,16,128]{2,1,0:T(8,128)S(1)} %copy-done.3), custom_call_target="tpu_custom_call" | custom-call | tf_op jit(solution)/shard_map/inner/pallas_call | solution.py:156
  24.5 1.1 %collective-permute-done.9.other = f32[7,4,16,128]{3,2,1,0:T(8,128)S(1)} collective-permute-done((f32[7,4,16,128]{3,2,1,0:T(8,128)S(1)}, f32[7,4,16,128]{3,2,1,0:T(8,128)S(1)}, u32[]{:S(2)}, u32[]{:S(2)}) %collective-permute-start.9) | collective-permute-done | bytes 229408 | tf_op jit(solution)/shard_map/ppermute | solution.py:142
  25.6 1.1 %outer.1 = f32[1,4,6,16,128]{4,3,2,1,0:T(8,128)} custom-call(f32[1,4,6,16,128]{4,3,2,1,0:T(8,128)S(1)} %get-tuple-element.15.own, f32[6,16,128]{2,1,0:T(8,128)S(1)} %copy-done.1, f32[6,16,128]{2,1,0:T(8,128)S(1)} %copy-done.2, f32[6,16,128]{2,1,0:T(8,128)S(1)} %copy-done.3, f32[7,4,16,128]{3,2,1,0:T(8,128)S(1)} %collective-permute-done.9.other, ...), custom_call_target="tpu_custom_call" | custom-call | tf_op jit(solution)/shard_map/outer/pallas_call | solution.py:156
  (10 shorter events, 0.0 us)
Async XLA Ops:
  0.0 12.0 %collective-permute-start.2 = (f32[1,4,6,16,128]{4,3,2,1,0:T(8,128)}, f32[1,4,6,16,128]{4,3,2,1,0:T(8,128)S(1)}, u32[]{:S(2)}, u32[]{:S(2)}) collective-permute-start(f32[1,4,6,16,128]{4,3,2,1,0:T(8,128)} %refs_0_.3), channel_id=1, source_target_pairs={{0,6},{1,17},{2,4},{3,19},{4,2},{5,21},{6,0},{7,23},{8,14},{9,25},... | collective-permute-start | bytes 589832 | tf_op jit(solution)/shard_map/ppermute | solution.py:266
  3.9 8.1 %collective-permute-start.1 = (f32[1,4,6,16,128]{4,3,2,1,0:T(8,128)}, f32[1,4,6,16,128]{4,3,2,1,0:T(8,128)S(1)}, u32[]{:S(2)}, u32[]{:S(2)}) collective-permute-start(f32[1,4,6,16,128]{4,3,2,1,0:T(8,128)} %refs_0_.3), channel_id=1, source_target_pairs={{0,2},{1,25},{2,0},{3,27},{4,6},{5,29},{6,4},{7,31},{8,10},{9,17},... | collective-permute-start | bytes 589832 | tf_op jit(solution)/shard_map/ppermute | solution.py:266
  4.4 7.6 %collective-permute-start = (f32[1,4,6,16,128]{4,3,2,1,0:T(8,128)}, f32[1,4,6,16,128]{4,3,2,1,0:T(8,128)S(1)}, u32[]{:S(2)}, u32[]{:S(2)}) collective-permute-start(f32[1,4,6,16,128]{4,3,2,1,0:T(8,128)} %refs_0_.3), channel_id=1, source_target_pairs={{0,4},{1,9},{2,6},{3,11},{4,0},{5,13},{6,2},{7,15},{8,12},{9,1},{1... | collective-permute-start | bytes 589832 | tf_op jit(solution)/shard_map/ppermute | solution.py:266
  5.1 6.9 %copy-start = (f32[1,4,6,16,128]{4,3,2,1,0:T(8,128)S(1)}, f32[1,4,6,16,128]{4,3,2,1,0:T(8,128)}, u32[]{:S(2)}) copy-start(f32[1,4,6,16,128]{4,3,2,1,0:T(8,128)} %refs_0_.3) | copy-start | bytes 589828
  5.1 5.4 %collective-permute-start.3 = (s32[8,128]{1,0:T(8,128)S(1)}, s32[8,128]{1,0:T(8,128)S(1)}, u32[]{:S(2)}, u32[]{:S(2)}) collective-permute-start(s32[8,128]{1,0:T(8,128)S(1)} %first_wishes.1.refs_4_), channel_id=1, source_target_pairs={{0,16},{1,3},{2,18},{3,1},{4,20},{5,7},{6,22},{7,5},{8,24},{9,11},... | collective-permute-start | bytes 12296 | tf_op jit(solution)/shard_map/ppermute | solution.py:266
  8.3 3.7 %collective-permute-start.4 = (s32[8,128]{1,0:T(8,128)S(1)}, s32[8,128]{1,0:T(8,128)S(1)}, u32[]{:S(2)}, u32[]{:S(2)}) collective-permute-start(s32[8,128]{1,0:T(8,128)S(1)} %first_wishes.1.refs_4_), channel_id=1, source_target_pairs={{0,8},{1,5},{2,10},{3,7},{4,12},{5,1},{6,14},{7,3},{8,0},{9,13},{1... | collective-permute-start | bytes 12296 | tf_op jit(solution)/shard_map/ppermute | solution.py:266
  10.6 5.3 %collective-permute-start.7 = (s32[8,128]{1,0:T(8,128)S(1)}, s32[8,128]{1,0:T(8,128)S(1)}, u32[]{:S(2)}, u32[]{:S(2)}) collective-permute-start(s32[8,128]{1,0:T(8,128)S(1)} %collective-permute-done.3.refs_5_), channel_id=1, source_target_pairs={{0,8},{1,5},{2,10},{3,7},{4,12},{5,1},{6,14},{7,3},{8,0},{9,13},{1... | collective-permute-start | bytes 12296 | tf_op jit(solution)/shard_map/ppermute | solution.py:266
  12.1 8.8 %collective-permute-start.5 = (f32[1,4,6,16,128]{4,3,2,1,0:T(8,128)S(1)}, f32[1,4,6,16,128]{4,3,2,1,0:T(8,128)S(1)}, u32[]{:S(2)}, u32[]{:S(2)}) collective-permute-start(f32[1,4,6,16,128]{4,3,2,1,0:T(8,128)S(1)} %get-tuple-element.13), channel_id=1, source_target_pairs={{0,16},{1,3},{2,18},{3,1},{4,20},{5,7},{6,22},{7,5},{8,24},{9,11},... | collective-permute-start | bytes 589832 | tf_op jit(solution)/shard_map/ppermute | solution.py:266
  14.7 9.3 %copy-start.1 = (f32[6,16,128]{2,1,0:T(8,128)S(1)}, f32[6,16,128]{2,1,0:T(8,128)}, u32[]{:S(2)}) copy-start(f32[6,16,128]{2,1,0:T(8,128)} %d.3) | copy-start | bytes 147460
  14.7 9.3 %copy-start.2 = (f32[6,16,128]{2,1,0:T(8,128)S(1)}, f32[6,16,128]{2,1,0:T(8,128)}, u32[]{:S(2)}) copy-start(f32[6,16,128]{2,1,0:T(8,128)} %r.3) | copy-start | bytes 147460
  14.7 9.3 %copy-start.3 = (f32[6,16,128]{2,1,0:T(8,128)S(1)}, f32[6,16,128]{2,1,0:T(8,128)}, u32[]{:S(2)}) copy-start(f32[6,16,128]{2,1,0:T(8,128)} %p.3) | copy-start | bytes 147460
  14.7 6.8 %collective-permute-start.6 = (f32[1,4,6,16,128]{4,3,2,1,0:T(8,128)S(1)}, f32[1,4,6,16,128]{4,3,2,1,0:T(8,128)S(1)}, u32[]{:S(2)}, u32[]{:S(2)}) collective-permute-start(f32[1,4,6,16,128]{4,3,2,1,0:T(8,128)S(1)} %get-tuple-element.14), channel_id=1, source_target_pairs={{0,8},{1,5},{2,10},{3,7},{4,12},{5,1},{6,14},{7,3},{8,0},{9,13},{1... | collective-permute-start | bytes 589832 | tf_op jit(solution)/shard_map/ppermute | solution.py:266
  15.9 8.1 %collective-permute-start.8 = (f32[1,4,6,16,128]{4,3,2,1,0:T(8,128)S(1)}, f32[1,4,6,16,128]{4,3,2,1,0:T(8,128)S(1)}, u32[]{:S(2)}, u32[]{:S(2)}) collective-permute-start(f32[1,4,6,16,128]{4,3,2,1,0:T(8,128)S(1)} %choose.3), channel_id=1, source_target_pairs={{0,24},{1,7},{2,26},{3,5},{4,28},{5,3},{6,30},{7,1},{8,16},{9,15},... | collective-permute-start | bytes 589832 | tf_op jit(solution)/shard_map/ppermute | solution.py:266
  24.1 1.6 %collective-permute-start.9 = (f32[7,4,16,128]{3,2,1,0:T(8,128)S(1)}, f32[7,4,16,128]{3,2,1,0:T(8,128)S(1)}, u32[]{:S(2)}, u32[]{:S(2)}) collective-permute-start(f32[7,4,16,128]{3,2,1,0:T(8,128)S(1)} %get-tuple-element.16), channel_id=1, source_target_pairs={{0,1},{1,0},{2,3},{3,2},{4,5},{5,4},{6,7},{7,6},{8,9},{9,8},{10,11... | collective-permute-start | bytes 688136 | tf_op jit(solution)/shard_map/ppermute | solution.py:142

commit v5 on v4

--- a/solution.py
+++ b/solution.py
@@ -43,7 +43,7 @@
     melting = reacts * (h - 0.5 * c)
     return (
         m - transport(m, m_up, m_low) + melting,
-        v + 0.2 * (permeab * jnp.tanh(m) - v) + 0.1 * laplace(v, v_up, v_low),
+        0.2 * (permeab * jnp.tanh(m) + v) + 0.1 * (v_up + v_low + neighbours(v)),
         h - transport(h, h_up, h_low) + diffuse * laplace(h, h_up, h_low) - 0.5 * melting,
         c - transport(c, c_up, c_low) + diffuse * laplace(c, c_up, c_low),
     )
@@ -108,8 +108,19 @@
                     border[step, q, layer - layers + 1] = values[q]
 
 
-def outer_kernel(cells, own, d, r, p, other, head, border, out, state):
+def outer_kernel(cells, own, d, r, p, other, head, border, out, state, result, sems):
     sign = sign_of_order()
+    copies = []
+
+    def leave(layer, values):
+        for q in range(4):
+            result[q, layer - 1] = values[q]
+        to = out.at[0, :, from_end(cells, layer - 1)]
+        copies.append(pltpu.make_async_copy(result.at[:, layer - 1], to, sems.at[layer - 1]))
+        copies[-1].start()
+
+    for layer in range(1, cells - STEPS + 1):
+        leave(layer, [head[q, layer - 1] for q in range(4)])
     for q in range(4):
         for i in range(2):
             state[0, q, i] = own[0, q, from_end(cells, cells - 2 + i)]
@@ -117,8 +128,6 @@
                 state[step, q, i] = border[step - 1, q, i]
         for i in range(STEPS):
             state[0, q, 2 + i] = other[q, from_end(STEPS, i)]
-        for i in range(cells - STEPS):
-            out[0, q, from_end(cells, i)] = head[q, i]
     for step in range(STEPS):
         for i in range(1, 1 + STEPS):
             layer = cells - 1 - step + i
@@ -129,11 +138,13 @@
                 at = from_end(STEPS, layer - cells - 1)
                 coefs = other[4, at], other[5, at], other[6, at]
             values = layer_step(lambda q, j: state[step, q, j], i, sign, *coefs)
+            if step == STEPS - 1:
+                leave(layer, values)
+                continue
             for q in range(4):
-                if step == STEPS - 1:
-                    out[0, q, from_end(cells, layer - 1)] = values[q]
-                else:
-                    state[step + 1, q, 1 + i] = values[q]
+                state[step + 1, q, 1 + i] = values[q]
+    for copy in copies:
+        copy.wait()
 
 
 def other_side(x, towards):
@@ -150,15 +161,18 @@
     result = jax.ShapeDtypeStruct(state.shape, jnp.float32)
 
     def layers(*lead):
-        return lead + (rows, columns)
-
-    def call(kernel, out_shape, scratch, *operands):
+        return jax.ShapeDtypeStruct(lead + (rows, columns), jnp.float32)
+
+    def held(*lead):
+        return pltpu.VMEM(lead + (rows, columns), jnp.float32)
+
+    def call(kernel, out_shape, scratch, *operands, space=VMEM):
         return pl.pallas_call(
             kernel,
             out_shape=out_shape,
             in_specs=[VMEM] * len(operands),
-            out_specs=jax.tree.map(lambda _: VMEM, out_shape),
-            scratch_shapes=[pltpu.VMEM(shape, jnp.float32) for shape in scratch],
+            out_specs=jax.tree.map(lambda _: space, out_shape),
+            scratch_shapes=scratch,
             compiler_params=LIMIT,
             name=kernel.func.__name__.removesuffix("_kernel"),
         )(*operands)
@@ -166,18 +180,19 @@
     if count == 2:
         other = other_side(edges[0], 1)
         parts = (
-            jax.ShapeDtypeStruct(layers(4, max(cells - STEPS, 1)), jnp.float32),
-            jax.ShapeDtypeStruct(layers(STEPS - 1, 4, 2), jnp.float32),
+            layers(4, max(cells - STEPS, 1)),
+            layers(STEPS - 1, 4, 2),
         )
         inner = functools.partial(inner_kernel, cells)
-        head, border = call(inner, parts, [layers(4, cells + 1)] * 2, state, *coefs)
+        head, border = call(inner, parts, [held(4, cells + 1)] * 2, state, *coefs)
         outer = functools.partial(outer_kernel, cells)
-        return call(outer, result, [layers(STEPS, 4, STEPS + 2)], state, *coefs, other, head, border)
+        scratch = [held(STEPS, 4, STEPS + 2), held(4, cells), pltpu.SemaphoreType.DMA((cells,))]
+        return call(outer, result, scratch, state, *coefs, other, head, border, space=pl.BlockSpec(memory_space=pl.ANY))
     window = cells + 2 * STEPS + 2
     return call(
         functools.partial(forecast_kernel, cells, count),
         result,
-        [layers(4, window), layers(4, window), layers(3, window)],
+        [held(4, window), held(4, window), held(3, window)],
         state,
         *coefs,
         other_side(edges[1], 1),

time: 26.9 us -> 26.8 us (level)
  no operation moved by 1% of the time
where the time goes in v5:
time: 26.8 us; the launch traced here: 26.7 us
  starting transfers between devices  16 us (60%)
  waiting for transfers between devices  8.28 us (31%)
  Pallas kernels  1.6 us (6%)
  between operations  0.72 us (3%)
    ppermute x9, starting transfers between devices, swap(): return lax.ppermute(x, ('dom', 'depth'), pairs)  16 us
    ppermute x9, waiting for transfers between devices, swap(): return lax.ppermute(x, ('dom', 'depth'), pairs)  7.18 us
    pallas_call x2, Pallas kernels, call(): pl.pallas_call(kernel, out_shape=out_shape, in_specs=[VMEM] * len(operand...  1.39 us
    ppermute x1, waiting for transfers between devices, other_side(): return lax.ppermute(x, 'depth', [(0, 1), (1, 0)])  1.1 us
  transfers between devices with their start and end apart: 10, of which 6 were waited for; matrix products, arithmetic and copies ran while one was open for 0% of the time, Pallas kernels for 2%

profile of v5, /device:TPU:0, one launch (start us, length us, event | category | flops | bytes accessed | tf_op | source)
XLA Modules:
  0.0 26.7 jit_solution(14625126886643112718)
XLA Ops:
  0.0 3.9 %collective-permute-start.2 = (f32[1,4,6,16,128]{4,3,2,1,0:T(8,128)}, f32[1,4,6,16,128]{4,3,2,1,0:T(8,128)S(1)}, u32[]{:S(2)}, u32[]{:S(2)}) collective-permute-start(f32[1,4,6,16,128]{4,3,2,1,0:T(8,128)} %refs_0_.3), channel_id=1, source_target_pairs={{0,6},{1,17},{2,4},{3,19},{4,2},{5,21},{6,0},{7,23},{8,14},{9,25},... | collective-permute-start | bytes 589832 | tf_op jit(solution)/shard_map/ppermute | solution.py:281
  3.9 0.5 %collective-permute-start.1 = (f32[1,4,6,16,128]{4,3,2,1,0:T(8,128)}, f32[1,4,6,16,128]{4,3,2,1,0:T(8,128)S(1)}, u32[]{:S(2)}, u32[]{:S(2)}) collective-permute-start(f32[1,4,6,16,128]{4,3,2,1,0:T(8,128)} %refs_0_.3), channel_id=1, source_target_pairs={{0,2},{1,25},{2,0},{3,27},{4,6},{5,29},{6,4},{7,31},{8,10},{9,17},... | collective-permute-start | bytes 589832 | tf_op jit(solution)/shard_map/ppermute | solution.py:281
  4.4 0.0 collective-permute-start
  5.1 3.1 %collective-permute-start.3 = (s32[8,128]{1,0:T(8,128)S(1)}, s32[8,128]{1,0:T(8,128)S(1)}, u32[]{:S(2)}, u32[]{:S(2)}) collective-permute-start(s32[8,128]{1,0:T(8,128)S(1)} %first_wishes.1.refs_4_), channel_id=1, source_target_pairs={{0,16},{1,3},{2,18},{3,1},{4,20},{5,7},{6,22},{7,5},{8,24},{9,11},... | collective-permute-start | bytes 12296 | tf_op jit(solution)/shard_map/ppermute | solution.py:281
  8.3 1.6 %collective-permute-start.4 = (s32[8,128]{1,0:T(8,128)S(1)}, s32[8,128]{1,0:T(8,128)S(1)}, u32[]{:S(2)}, u32[]{:S(2)}) collective-permute-start(s32[8,128]{1,0:T(8,128)S(1)} %first_wishes.1.refs_4_), channel_id=1, source_target_pairs={{0,8},{1,5},{2,10},{3,7},{4,12},{5,1},{6,14},{7,3},{8,0},{9,13},{1... | collective-permute-start | bytes 12296 | tf_op jit(solution)/shard_map/ppermute | solution.py:281
  9.8 0.7 %collective-permute-done.3.refs_5_ = s32[8,128]{1,0:T(8,128)S(1)} collective-permute-done((s32[8,128]{1,0:T(8,128)S(1)}, s32[8,128]{1,0:T(8,128)S(1)}, u32[]{:S(2)}, u32[]{:S(2)}) %collective-permute-start.3) | collective-permute-done | bytes 4128 | tf_op jit(solution)/shard_map/ppermute | solution.py:281
  10.6 1.3 %collective-permute-start.7 = (s32[8,128]{1,0:T(8,128)S(1)}, s32[8,128]{1,0:T(8,128)S(1)}, u32[]{:S(2)}, u32[]{:S(2)}) collective-permute-start(s32[8,128]{1,0:T(8,128)S(1)} %collective-permute-done.3.refs_5_), channel_id=1, source_target_pairs={{0,8},{1,5},{2,10},{3,7},{4,12},{5,1},{6,14},{7,3},{8,0},{9,13},{1... | collective-permute-start | bytes 12296 | tf_op jit(solution)/shard_map/ppermute | solution.py:281
  11.9 0.1 collective-permute-done.4.refs_6_
  12.0 0.0 collective-permute-done.2.refs_3_
  12.0 0.0 collective-permute-done.1.refs_2_
  12.0 0.0 collective-permute-done.refs_1_
  12.0 0.1 choose.2
  12.1 2.6 %collective-permute-start.5 = (f32[1,4,6,16,128]{4,3,2,1,0:T(8,128)S(1)}, f32[1,4,6,16,128]{4,3,2,1,0:T(8,128)S(1)}, u32[]{:S(2)}, u32[]{:S(2)}) collective-permute-start(f32[1,4,6,16,128]{4,3,2,1,0:T(8,128)S(1)} %get-tuple-element.13), channel_id=1, source_target_pairs={{0,16},{1,3},{2,18},{3,1},{4,20},{5,7},{6,22},{7,5},{8,24},{9,11},... | collective-permute-start | bytes 589832 | tf_op jit(solution)/shard_map/ppermute | solution.py:281
  14.7 1.1 %collective-permute-start.6 = (f32[1,4,6,16,128]{4,3,2,1,0:T(8,128)S(1)}, f32[1,4,6,16,128]{4,3,2,1,0:T(8,128)S(1)}, u32[]{:S(2)}, u32[]{:S(2)}) collective-permute-start(f32[1,4,6,16,128]{4,3,2,1,0:T(8,128)S(1)} %get-tuple-element.14), channel_id=1, source_target_pairs={{0,8},{1,5},{2,10},{3,7},{4,12},{5,1},{6,14},{7,3},{8,0},{9,13},{1... | collective-permute-start | bytes 589832 | tf_op jit(solution)/shard_map/ppermute | solution.py:281
  15.8 0.1 choose.3
  15.9 1.8 %collective-permute-start.8 = (f32[1,4,6,16,128]{4,3,2,1,0:T(8,128)S(1)}, f32[1,4,6,16,128]{4,3,2,1,0:T(8,128)S(1)}, u32[]{:S(2)}, u32[]{:S(2)}) collective-permute-start(f32[1,4,6,16,128]{4,3,2,1,0:T(8,128)S(1)} %choose.3), channel_id=1, source_target_pairs={{0,24},{1,7},{2,26},{3,5},{4,28},{5,3},{6,30},{7,1},{8,16},{9,15},... | collective-permute-start | bytes 589832 | tf_op jit(solution)/shard_map/ppermute | solution.py:281
  17.7 3.3 %collective-permute-done.5.refs_1_ = f32[1,4,6,16,128]{4,3,2,1,0:T(8,128)S(1)} collective-permute-done((f32[1,4,6,16,128]{4,3,2,1,0:T(8,128)S(1)}, f32[1,4,6,16,128]{4,3,2,1,0:T(8,128)S(1)}, u32[]{:S(2)}, u32[]{:S(2)}) %collective-permute-start.5) | collective-permute-done | bytes 196640 | tf_op jit(solution)/shard_map/ppermute | solution.py:281
  20.9 0.5 %collective-permute-done.6.refs_2_ = f32[1,4,6,16,128]{4,3,2,1,0:T(8,128)S(1)} collective-permute-done((f32[1,4,6,16,128]{4,3,2,1,0:T(8,128)S(1)}, f32[1,4,6,16,128]{4,3,2,1,0:T(8,128)S(1)}, u32[]{:S(2)}, u32[]{:S(2)}) %collective-permute-start.6) | collective-permute-done | bytes 196640 | tf_op jit(solution)/shard_map/ppermute | solution.py:281
  21.5 2.5 %collective-permute-done.8.refs_3_ = f32[1,4,6,16,128]{4,3,2,1,0:T(8,128)S(1)} collective-permute-done((f32[1,4,6,16,128]{4,3,2,1,0:T(8,128)S(1)}, f32[1,4,6,16,128]{4,3,2,1,0:T(8,128)S(1)}, u32[]{:S(2)}, u32[]{:S(2)}) %collective-permute-start.8) | collective-permute-done | bytes 196640 | tf_op jit(solution)/shard_map/ppermute | solution.py:281
  24.0 0.1 settle.1
  24.1 0.1 collective-permute-start.9
  24.2 0.4 %inner.1 = (f32[4,2,16,128]{3,2,1,0:T(8,128)S(1)}, f32[3,4,2,16,128]{4,3,2,1,0:T(8,128)S(1)}) custom-call(f32[1,4,6,16,128]{4,3,2,1,0:T(8,128)S(1)} %get-tuple-element.15.own, f32[6,16,128]{2,1,0:T(8,128)S(1)} %copy-done.1, f32[6,16,128]{2,1,0:T(8,128)S(1)} %copy-done.2, f32[6,16,128]{2,1,0:T(8,128)S(1)} %copy-done.3), custom_call_target="tpu_custom_call" | custom-call | tf_op jit(solution)/shard_map/inner/pallas_call | solution.py:170
  24.5 1.1 %collective-permute-done.9.other = f32[7,4,16,128]{3,2,1,0:T(8,128)S(1)} collective-permute-done((f32[7,4,16,128]{3,2,1,0:T(8,128)S(1)}, f32[7,4,16,128]{3,2,1,0:T(8,128)S(1)}, u32[]{:S(2)}, u32[]{:S(2)}) %collective-permute-start.9) | collective-permute-done | bytes 229408 | tf_op jit(solution)/shard_map/ppermute | solution.py:153
  25.6 1.0 %outer.1 = f32[1,4,6,16,128]{4,3,2,1,0:T(8,128)} custom-call(f32[1,4,6,16,128]{4,3,2,1,0:T(8,128)S(1)} %get-tuple-element.15.own, f32[6,16,128]{2,1,0:T(8,128)S(1)} %copy-done.1, f32[6,16,128]{2,1,0:T(8,128)S(1)} %copy-done.2, f32[6,16,128]{2,1,0:T(8,128)S(1)} %copy-done.3, f32[7,4,16,128]{3,2,1,0:T(8,128)S(1)} %collective-permute-done.9.other, ...), custom_call_target="tpu_custom_call" | custom-call | tf_op jit(solution)/shard_map/outer/pallas_call | solution.py:170
  (10 shorter events, 0.0 us)
Async XLA Ops:
  0.0 12.0 %collective-permute-start.2 = (f32[1,4,6,16,128]{4,3,2,1,0:T(8,128)}, f32[1,4,6,16,128]{4,3,2,1,0:T(8,128)S(1)}, u32[]{:S(2)}, u32[]{:S(2)}) collective-permute-start(f32[1,4,6,16,128]{4,3,2,1,0:T(8,128)} %refs_0_.3), channel_id=1, source_target_pairs={{0,6},{1,17},{2,4},{3,19},{4,2},{5,21},{6,0},{7,23},{8,14},{9,25},... | collective-permute-start | bytes 589832 | tf_op jit(solution)/shard_map/ppermute | solution.py:281
  3.9 8.1 %collective-permute-start.1 = (f32[1,4,6,16,128]{4,3,2,1,0:T(8,128)}, f32[1,4,6,16,128]{4,3,2,1,0:T(8,128)S(1)}, u32[]{:S(2)}, u32[]{:S(2)}) collective-permute-start(f32[1,4,6,16,128]{4,3,2,1,0:T(8,128)} %refs_0_.3), channel_id=1, source_target_pairs={{0,2},{1,25},{2,0},{3,27},{4,6},{5,29},{6,4},{7,31},{8,10},{9,17},... | collective-permute-start | bytes 589832 | tf_op jit(solution)/shard_map/ppermute | solution.py:281
  4.4 7.6 %collective-permute-start = (f32[1,4,6,16,128]{4,3,2,1,0:T(8,128)}, f32[1,4,6,16,128]{4,3,2,1,0:T(8,128)S(1)}, u32[]{:S(2)}, u32[]{:S(2)}) collective-permute-start(f32[1,4,6,16,128]{4,3,2,1,0:T(8,128)} %refs_0_.3), channel_id=1, source_target_pairs={{0,4},{1,9},{2,6},{3,11},{4,0},{5,13},{6,2},{7,15},{8,12},{9,1},{1... | collective-permute-start | bytes 589832 | tf_op jit(solution)/shard_map/ppermute | solution.py:281
  5.1 6.9 %copy-start = (f32[1,4,6,16,128]{4,3,2,1,0:T(8,128)S(1)}, f32[1,4,6,16,128]{4,3,2,1,0:T(8,128)}, u32[]{:S(2)}) copy-start(f32[1,4,6,16,128]{4,3,2,1,0:T(8,128)} %refs_0_.3) | copy-start | bytes 589828
  5.1 5.4 %collective-permute-start.3 = (s32[8,128]{1,0:T(8,128)S(1)}, s32[8,128]{1,0:T(8,128)S(1)}, u32[]{:S(2)}, u32[]{:S(2)}) collective-permute-start(s32[8,128]{1,0:T(8,128)S(1)} %first_wishes.1.refs_4_), channel_id=1, source_target_pairs={{0,16},{1,3},{2,18},{3,1},{4,20},{5,7},{6,22},{7,5},{8,24},{9,11},... | collective-permute-start | bytes 12296 | tf_op jit(solution)/shard_map/ppermute | solution.py:281
  8.3 3.7 %collective-permute-start.4 = (s32[8,128]{1,0:T(8,128)S(1)}, s32[8,128]{1,0:T(8,128)S(1)}, u32[]{:S(2)}, u32[]{:S(2)}) collective-permute-start(s32[8,128]{1,0:T(8,128)S(1)} %first_wishes.1.refs_4_), channel_id=1, source_target_pairs={{0,8},{1,5},{2,10},{3,7},{4,12},{5,1},{6,14},{7,3},{8,0},{9,13},{1... | collective-permute-start | bytes 12296 | tf_op jit(solution)/shard_map/ppermute | solution.py:281
  10.6 5.3 %collective-permute-start.7 = (s32[8,128]{1,0:T(8,128)S(1)}, s32[8,128]{1,0:T(8,128)S(1)}, u32[]{:S(2)}, u32[]{:S(2)}) collective-permute-start(s32[8,128]{1,0:T(8,128)S(1)} %collective-permute-done.3.refs_5_), channel_id=1, source_target_pairs={{0,8},{1,5},{2,10},{3,7},{4,12},{5,1},{6,14},{7,3},{8,0},{9,13},{1... | collective-permute-start | bytes 12296 | tf_op jit(solution)/shard_map/ppermute | solution.py:281
  12.1 8.8 %collective-permute-start.5 = (f32[1,4,6,16,128]{4,3,2,1,0:T(8,128)S(1)}, f32[1,4,6,16,128]{4,3,2,1,0:T(8,128)S(1)}, u32[]{:S(2)}, u32[]{:S(2)}) collective-permute-start(f32[1,4,6,16,128]{4,3,2,1,0:T(8,128)S(1)} %get-tuple-element.13), channel_id=1, source_target_pairs={{0,16},{1,3},{2,18},{3,1},{4,20},{5,7},{6,22},{7,5},{8,24},{9,11},... | collective-permute-start | bytes 589832 | tf_op jit(solution)/shard_map/ppermute | solution.py:281
  14.7 9.3 %copy-start.1 = (f32[6,16,128]{2,1,0:T(8,128)S(1)}, f32[6,16,128]{2,1,0:T(8,128)}, u32[]{:S(2)}) copy-start(f32[6,16,128]{2,1,0:T(8,128)} %d.3) | copy-start | bytes 147460
  14.7 9.3 %copy-start.2 = (f32[6,16,128]{2,1,0:T(8,128)S(1)}, f32[6,16,128]{2,1,0:T(8,128)}, u32[]{:S(2)}) copy-start(f32[6,16,128]{2,1,0:T(8,128)} %r.3) | copy-start | bytes 147460
  14.7 9.3 %copy-start.3 = (f32[6,16,128]{2,1,0:T(8,128)S(1)}, f32[6,16,128]{2,1,0:T(8,128)}, u32[]{:S(2)}) copy-start(f32[6,16,128]{2,1,0:T(8,128)} %p.3) | copy-start | bytes 147460
  14.7 6.8 %collective-permute-start.6 = (f32[1,4,6,16,128]{4,3,2,1,0:T(8,128)S(1)}, f32[1,4,6,16,128]{4,3,2,1,0:T(8,128)S(1)}, u32[]{:S(2)}, u32[]{:S(2)}) collective-permute-start(f32[1,4,6,16,128]{4,3,2,1,0:T(8,128)S(1)} %get-tuple-element.14), channel_id=1, source_target_pairs={{0,8},{1,5},{2,10},{3,7},{4,12},{5,1},{6,14},{7,3},{8,0},{9,13},{1... | collective-permute-start | bytes 589832 | tf_op jit(solution)/shard_map/ppermute | solution.py:281
  15.9 8.1 %collective-permute-start.8 = (f32[1,4,6,16,128]{4,3,2,1,0:T(8,128)S(1)}, f32[1,4,6,16,128]{4,3,2,1,0:T(8,128)S(1)}, u32[]{:S(2)}, u32[]{:S(2)}) collective-permute-start(f32[1,4,6,16,128]{4,3,2,1,0:T(8,128)S(1)} %choose.3), channel_id=1, source_target_pairs={{0,24},{1,7},{2,26},{3,5},{4,28},{5,3},{6,30},{7,1},{8,16},{9,15},... | collective-permute-start | bytes 589832 | tf_op jit(solution)/shard_map/ppermute | solution.py:281
  24.1 1.6 %collective-permute-start.9 = (f32[7,4,16,128]{3,2,1,0:T(8,128)S(1)}, f32[7,4,16,128]{3,2,1,0:T(8,128)S(1)}, u32[]{:S(2)}, u32[]{:S(2)}) collective-permute-start(f32[7,4,16,128]{3,2,1,0:T(8,128)S(1)} %get-tuple-element.16), channel_id=1, source_target_pairs={{0,1},{1,0},{2,3},{3,2},{4,5},{5,4},{6,7},{7,6},{8,9},{9,8},{10,11... | collective-permute-start | bytes 688136 | tf_op jit(solution)/shard_map/ppermute | solution.py:153

commit v6 on v4

--- a/solution.py
+++ b/solution.py
@@ -43,7 +43,7 @@
     melting = reacts * (h - 0.5 * c)
     return (
         m - transport(m, m_up, m_low) + melting,
-        v + 0.2 * (permeab * jnp.tanh(m) - v) + 0.1 * laplace(v, v_up, v_low),
+        0.2 * (permeab * jnp.tanh(m) + v) + 0.1 * (v_up + v_low + neighbours(v)),
         h - transport(h, h_up, h_low) + diffuse * laplace(h, h_up, h_low) - 0.5 * melting,
         c - transport(c, c_up, c_low) + diffuse * laplace(c, c_up, c_low),
     )
@@ -244,8 +244,13 @@
     )(*candidates, *wishes)
 
 
+def settle_order(sides):
+    return (1, *range(sides - 1, 1, -1))
+
+
 def settle_kernel(sides, pair, *refs):
     candidates, wishes, coefs = refs[:sides], refs[sides], refs[sides + 1 : sides + 4]
+    candidates = [candidates[(0, *settle_order(sides)).index(k)] for k in range(sides)]
     result, edges = refs[sides + 4], refs[sides + 5 :]
     masks = hop_masks(wishes[...], 1)
     for at in tiles(result.shape):
@@ -302,7 +307,7 @@
         out_specs=[VMEM] * (1 + len(edges)),
         compiler_params=LIMIT,
         name="settle",
-    )(sent[0], *(final[k] for k in far), wish, *coefs)
+    )(sent[0], *(final[k] for k in settle_order(sides)), wish, *coefs)
     return forecast(state, edges, coefs)
 
 

time: 26.9 us -> 26.9 us (level)
  no operation moved by 1% of the time
where the time goes in v6:
time: 26.9 us; the launch traced here: 26.7 us
  starting transfers between devices  16 us (59%)
  waiting for transfers between devices  8.28 us (31%)
  Pallas kernels  1.64 us (6%)
  between operations  0.72 us (3%)
    ppermute x9, starting transfers between devices, swap(): return lax.ppermute(x, ('dom', 'depth'), pairs)  16 us
    ppermute x9, waiting for transfers between devices, swap(): return lax.ppermute(x, ('dom', 'depth'), pairs)  7.18 us
    pallas_call x2, Pallas kernels, call(): pl.pallas_call(kernel, out_shape=out_shape, in_specs=[VMEM] * len(operand...  1.44 us
    ppermute x1, waiting for transfers between devices, other_side(): return lax.ppermute(x, 'depth', [(0, 1), (1, 0)])  1.1 us
  transfers between devices with their start and end apart: 10, of which 6 were waited for; matrix products, arithmetic and copies ran while one was open for 0% of the time, Pallas kernels for 2%

profile of v6, /device:TPU:0, one launch (start us, length us, event | category | flops | bytes accessed | tf_op | source)
XLA Modules:
  0.0 26.7 jit_solution(15053159934510405929)
XLA Ops:
  0.0 3.9 %collective-permute-start.2 = (f32[1,4,6,16,128]{4,3,2,1,0:T(8,128)}, f32[1,4,6,16,128]{4,3,2,1,0:T(8,128)S(1)}, u32[]{:S(2)}, u32[]{:S(2)}) collective-permute-start(f32[1,4,6,16,128]{4,3,2,1,0:T(8,128)} %refs_0_.3), channel_id=1, source_target_pairs={{0,6},{1,17},{2,4},{3,19},{4,2},{5,21},{6,0},{7,23},{8,14},{9,25},... | collective-permute-start | bytes 589832 | tf_op jit(solution)/shard_map/ppermute | solution.py:271
  3.9 0.5 %collective-permute-start.1 = (f32[1,4,6,16,128]{4,3,2,1,0:T(8,128)}, f32[1,4,6,16,128]{4,3,2,1,0:T(8,128)S(1)}, u32[]{:S(2)}, u32[]{:S(2)}) collective-permute-start(f32[1,4,6,16,128]{4,3,2,1,0:T(8,128)} %refs_0_.3), channel_id=1, source_target_pairs={{0,2},{1,25},{2,0},{3,27},{4,6},{5,29},{6,4},{7,31},{8,10},{9,17},... | collective-permute-start | bytes 589832 | tf_op jit(solution)/shard_map/ppermute | solution.py:271
  4.4 0.0 collective-permute-start
  5.1 3.1 %collective-permute-start.3 = (s32[8,128]{1,0:T(8,128)S(1)}, s32[8,128]{1,0:T(8,128)S(1)}, u32[]{:S(2)}, u32[]{:S(2)}) collective-permute-start(s32[8,128]{1,0:T(8,128)S(1)} %first_wishes.1.refs_4_), channel_id=1, source_target_pairs={{0,16},{1,3},{2,18},{3,1},{4,20},{5,7},{6,22},{7,5},{8,24},{9,11},... | collective-permute-start | bytes 12296 | tf_op jit(solution)/shard_map/ppermute | solution.py:271
  8.3 1.6 %collective-permute-start.4 = (s32[8,128]{1,0:T(8,128)S(1)}, s32[8,128]{1,0:T(8,128)S(1)}, u32[]{:S(2)}, u32[]{:S(2)}) collective-permute-start(s32[8,128]{1,0:T(8,128)S(1)} %first_wishes.1.refs_4_), channel_id=1, source_target_pairs={{0,8},{1,5},{2,10},{3,7},{4,12},{5,1},{6,14},{7,3},{8,0},{9,13},{1... | collective-permute-start | bytes 12296 | tf_op jit(solution)/shard_map/ppermute | solution.py:271
  9.8 0.7 %collective-permute-done.3.refs_5_ = s32[8,128]{1,0:T(8,128)S(1)} collective-permute-done((s32[8,128]{1,0:T(8,128)S(1)}, s32[8,128]{1,0:T(8,128)S(1)}, u32[]{:S(2)}, u32[]{:S(2)}) %collective-permute-start.3) | collective-permute-done | bytes 4128 | tf_op jit(solution)/shard_map/ppermute | solution.py:271
  10.6 1.3 %collective-permute-start.6 = (s32[8,128]{1,0:T(8,128)S(1)}, s32[8,128]{1,0:T(8,128)S(1)}, u32[]{:S(2)}, u32[]{:S(2)}) collective-permute-start(s32[8,128]{1,0:T(8,128)S(1)} %collective-permute-done.3.refs_5_), channel_id=1, source_target_pairs={{0,8},{1,5},{2,10},{3,7},{4,12},{5,1},{6,14},{7,3},{8,0},{9,13},{1... | collective-permute-start | bytes 12296 | tf_op jit(solution)/shard_map/ppermute | solution.py:271
  11.9 0.1 collective-permute-done.4.refs_6_
  12.0 0.0 collective-permute-done.2.refs_3_
  12.0 0.0 collective-permute-done.1.refs_2_
  12.0 0.0 collective-permute-done.refs_1_
  12.0 0.1 choose.2
  12.1 2.6 %collective-permute-start.5 = (f32[1,4,6,16,128]{4,3,2,1,0:T(8,128)S(1)}, f32[1,4,6,16,128]{4,3,2,1,0:T(8,128)S(1)}, u32[]{:S(2)}, u32[]{:S(2)}) collective-permute-start(f32[1,4,6,16,128]{4,3,2,1,0:T(8,128)S(1)} %get-tuple-element.13), channel_id=1, source_target_pairs={{0,16},{1,3},{2,18},{3,1},{4,20},{5,7},{6,22},{7,5},{8,24},{9,11},... | collective-permute-start | bytes 589832 | tf_op jit(solution)/shard_map/ppermute | solution.py:271
  14.7 1.1 %collective-permute-start.8 = (f32[1,4,6,16,128]{4,3,2,1,0:T(8,128)S(1)}, f32[1,4,6,16,128]{4,3,2,1,0:T(8,128)S(1)}, u32[]{:S(2)}, u32[]{:S(2)}) collective-permute-start(f32[1,4,6,16,128]{4,3,2,1,0:T(8,128)S(1)} %get-tuple-element.14), channel_id=1, source_target_pairs={{0,8},{1,5},{2,10},{3,7},{4,12},{5,1},{6,14},{7,3},{8,0},{9,13},{1... | collective-permute-start | bytes 589832 | tf_op jit(solution)/shard_map/ppermute | solution.py:271
  15.8 0.1 choose.3
  15.9 1.8 %collective-permute-start.7 = (f32[1,4,6,16,128]{4,3,2,1,0:T(8,128)S(1)}, f32[1,4,6,16,128]{4,3,2,1,0:T(8,128)S(1)}, u32[]{:S(2)}, u32[]{:S(2)}) collective-permute-start(f32[1,4,6,16,128]{4,3,2,1,0:T(8,128)S(1)} %choose.3), channel_id=1, source_target_pairs={{0,24},{1,7},{2,26},{3,5},{4,28},{5,3},{6,30},{7,1},{8,16},{9,15},... | collective-permute-start | bytes 589832 | tf_op jit(solution)/shard_map/ppermute | solution.py:271
  17.7 3.3 %collective-permute-done.5.refs_1_ = f32[1,4,6,16,128]{4,3,2,1,0:T(8,128)S(1)} collective-permute-done((f32[1,4,6,16,128]{4,3,2,1,0:T(8,128)S(1)}, f32[1,4,6,16,128]{4,3,2,1,0:T(8,128)S(1)}, u32[]{:S(2)}, u32[]{:S(2)}) %collective-permute-start.5) | collective-permute-done | bytes 196640 | tf_op jit(solution)/shard_map/ppermute | solution.py:271
  20.9 0.5 %collective-permute-done.8.refs_3_ = f32[1,4,6,16,128]{4,3,2,1,0:T(8,128)S(1)} collective-permute-done((f32[1,4,6,16,128]{4,3,2,1,0:T(8,128)S(1)}, f32[1,4,6,16,128]{4,3,2,1,0:T(8,128)S(1)}, u32[]{:S(2)}, u32[]{:S(2)}) %collective-permute-start.8) | collective-permute-done | bytes 196640 | tf_op jit(solution)/shard_map/ppermute | solution.py:271
  21.5 2.5 %collective-permute-done.7.refs_2_ = f32[1,4,6,16,128]{4,3,2,1,0:T(8,128)S(1)} collective-permute-done((f32[1,4,6,16,128]{4,3,2,1,0:T(8,128)S(1)}, f32[1,4,6,16,128]{4,3,2,1,0:T(8,128)S(1)}, u32[]{:S(2)}, u32[]{:S(2)}) %collective-permute-start.7) | collective-permute-done | bytes 196640 | tf_op jit(solution)/shard_map/ppermute | solution.py:271
  24.0 0.1 settle.1
  24.1 0.1 collective-permute-start.9
  24.2 0.4 %inner.1 = (f32[4,2,16,128]{3,2,1,0:T(8,128)S(1)}, f32[3,4,2,16,128]{4,3,2,1,0:T(8,128)S(1)}) custom-call(f32[1,4,6,16,128]{4,3,2,1,0:T(8,128)S(1)} %get-tuple-element.15.own, f32[6,16,128]{2,1,0:T(8,128)S(1)} %copy-done.1, f32[6,16,128]{2,1,0:T(8,128)S(1)} %copy-done.2, f32[6,16,128]{2,1,0:T(8,128)S(1)} %copy-done.3), custom_call_target="tpu_custom_call" | custom-call | tf_op jit(solution)/shard_map/inner/pallas_call | solution.py:156
  24.5 1.1 %collective-permute-done.9.other = f32[7,4,16,128]{3,2,1,0:T(8,128)S(1)} collective-permute-done((f32[7,4,16,128]{3,2,1,0:T(8,128)S(1)}, f32[7,4,16,128]{3,2,1,0:T(8,128)S(1)}, u32[]{:S(2)}, u32[]{:S(2)}) %collective-permute-start.9) | collective-permute-done | bytes 229408 | tf_op jit(solution)/shard_map/ppermute | solution.py:142
  25.6 1.1 %outer.1 = f32[1,4,6,16,128]{4,3,2,1,0:T(8,128)} custom-call(f32[1,4,6,16,128]{4,3,2,1,0:T(8,128)S(1)} %get-tuple-element.15.own, f32[6,16,128]{2,1,0:T(8,128)S(1)} %copy-done.1, f32[6,16,128]{2,1,0:T(8,128)S(1)} %copy-done.2, f32[6,16,128]{2,1,0:T(8,128)S(1)} %copy-done.3, f32[7,4,16,128]{3,2,1,0:T(8,128)S(1)} %collective-permute-done.9.other, ...), custom_call_target="tpu_custom_call" | custom-call | tf_op jit(solution)/shard_map/outer/pallas_call | solution.py:156
  (10 shorter events, 0.0 us)
Async XLA Ops:
  0.0 12.0 %collective-permute-start.2 = (f32[1,4,6,16,128]{4,3,2,1,0:T(8,128)}, f32[1,4,6,16,128]{4,3,2,1,0:T(8,128)S(1)}, u32[]{:S(2)}, u32[]{:S(2)}) collective-permute-start(f32[1,4,6,16,128]{4,3,2,1,0:T(8,128)} %refs_0_.3), channel_id=1, source_target_pairs={{0,6},{1,17},{2,4},{3,19},{4,2},{5,21},{6,0},{7,23},{8,14},{9,25},... | collective-permute-start | bytes 589832 | tf_op jit(solution)/shard_map/ppermute | solution.py:271
  3.9 8.1 %collective-permute-start.1 = (f32[1,4,6,16,128]{4,3,2,1,0:T(8,128)}, f32[1,4,6,16,128]{4,3,2,1,0:T(8,128)S(1)}, u32[]{:S(2)}, u32[]{:S(2)}) collective-permute-start(f32[1,4,6,16,128]{4,3,2,1,0:T(8,128)} %refs_0_.3), channel_id=1, source_target_pairs={{0,2},{1,25},{2,0},{3,27},{4,6},{5,29},{6,4},{7,31},{8,10},{9,17},... | collective-permute-start | bytes 589832 | tf_op jit(solution)/shard_map/ppermute | solution.py:271
  4.4 7.6 %collective-permute-start = (f32[1,4,6,16,128]{4,3,2,1,0:T(8,128)}, f32[1,4,6,16,128]{4,3,2,1,0:T(8,128)S(1)}, u32[]{:S(2)}, u32[]{:S(2)}) collective-permute-start(f32[1,4,6,16,128]{4,3,2,1,0:T(8,128)} %refs_0_.3), channel_id=1, source_target_pairs={{0,4},{1,9},{2,6},{3,11},{4,0},{5,13},{6,2},{7,15},{8,12},{9,1},{1... | collective-permute-start | bytes 589832 | tf_op jit(solution)/shard_map/ppermute | solution.py:271
  5.1 6.9 %copy-start = (f32[1,4,6,16,128]{4,3,2,1,0:T(8,128)S(1)}, f32[1,4,6,16,128]{4,3,2,1,0:T(8,128)}, u32[]{:S(2)}) copy-start(f32[1,4,6,16,128]{4,3,2,1,0:T(8,128)} %refs_0_.3) | copy-start | bytes 589828
  5.1 5.4 %collective-permute-start.3 = (s32[8,128]{1,0:T(8,128)S(1)}, s32[8,128]{1,0:T(8,128)S(1)}, u32[]{:S(2)}, u32[]{:S(2)}) collective-permute-start(s32[8,128]{1,0:T(8,128)S(1)} %first_wishes.1.refs_4_), channel_id=1, source_target_pairs={{0,16},{1,3},{2,18},{3,1},{4,20},{5,7},{6,22},{7,5},{8,24},{9,11},... | collective-permute-start | bytes 12296 | tf_op jit(solution)/shard_map/ppermute | solution.py:271
  8.3 3.7 %collective-permute-start.4 = (s32[8,128]{1,0:T(8,128)S(1)}, s32[8,128]{1,0:T(8,128)S(1)}, u32[]{:S(2)}, u32[]{:S(2)}) collective-permute-start(s32[8,128]{1,0:T(8,128)S(1)} %first_wishes.1.refs_4_), channel_id=1, source_target_pairs={{0,8},{1,5},{2,10},{3,7},{4,12},{5,1},{6,14},{7,3},{8,0},{9,13},{1... | collective-permute-start | bytes 12296 | tf_op jit(solution)/shard_map/ppermute | solution.py:271
  10.6 5.3 %collective-permute-start.6 = (s32[8,128]{1,0:T(8,128)S(1)}, s32[8,128]{1,0:T(8,128)S(1)}, u32[]{:S(2)}, u32[]{:S(2)}) collective-permute-start(s32[8,128]{1,0:T(8,128)S(1)} %collective-permute-done.3.refs_5_), channel_id=1, source_target_pairs={{0,8},{1,5},{2,10},{3,7},{4,12},{5,1},{6,14},{7,3},{8,0},{9,13},{1... | collective-permute-start | bytes 12296 | tf_op jit(solution)/shard_map/ppermute | solution.py:271
  12.1 8.8 %collective-permute-start.5 = (f32[1,4,6,16,128]{4,3,2,1,0:T(8,128)S(1)}, f32[1,4,6,16,128]{4,3,2,1,0:T(8,128)S(1)}, u32[]{:S(2)}, u32[]{:S(2)}) collective-permute-start(f32[1,4,6,16,128]{4,3,2,1,0:T(8,128)S(1)} %get-tuple-element.13), channel_id=1, source_target_pairs={{0,16},{1,3},{2,18},{3,1},{4,20},{5,7},{6,22},{7,5},{8,24},{9,11},... | collective-permute-start | bytes 589832 | tf_op jit(solution)/shard_map/ppermute | solution.py:271
  14.7 9.3 %copy-start.1 = (f32[6,16,128]{2,1,0:T(8,128)S(1)}, f32[6,16,128]{2,1,0:T(8,128)}, u32[]{:S(2)}) copy-start(f32[6,16,128]{2,1,0:T(8,128)} %d.3) | copy-start | bytes 147460
  14.7 9.3 %copy-start.2 = (f32[6,16,128]{2,1,0:T(8,128)S(1)}, f32[6,16,128]{2,1,0:T(8,128)}, u32[]{:S(2)}) copy-start(f32[6,16,128]{2,1,0:T(8,128)} %r.3) | copy-start | bytes 147460
  14.7 9.3 %copy-start.3 = (f32[6,16,128]{2,1,0:T(8,128)S(1)}, f32[6,16,128]{2,1,0:T(8,128)}, u32[]{:S(2)}) copy-start(f32[6,16,128]{2,1,0:T(8,128)} %p.3) | copy-start | bytes 147460
  14.7 6.8 %collective-permute-start.8 = (f32[1,4,6,16,128]{4,3,2,1,0:T(8,128)S(1)}, f32[1,4,6,16,128]{4,3,2,1,0:T(8,128)S(1)}, u32[]{:S(2)}, u32[]{:S(2)}) collective-permute-start(f32[1,4,6,16,128]{4,3,2,1,0:T(8,128)S(1)} %get-tuple-element.14), channel_id=1, source_target_pairs={{0,8},{1,5},{2,10},{3,7},{4,12},{5,1},{6,14},{7,3},{8,0},{9,13},{1... | collective-permute-start | bytes 589832 | tf_op jit(solution)/shard_map/ppermute | solution.py:271
  15.9 8.1 %collective-permute-start.7 = (f32[1,4,6,16,128]{4,3,2,1,0:T(8,128)S(1)}, f32[1,4,6,16,128]{4,3,2,1,0:T(8,128)S(1)}, u32[]{:S(2)}, u32[]{:S(2)}) collective-permute-start(f32[1,4,6,16,128]{4,3,2,1,0:T(8,128)S(1)} %choose.3), channel_id=1, source_target_pairs={{0,24},{1,7},{2,26},{3,5},{4,28},{5,3},{6,30},{7,1},{8,16},{9,15},... | collective-permute-start | bytes 589832 | tf_op jit(solution)/shard_map/ppermute | solution.py:271
  24.1 1.6 %collective-permute-start.9 = (f32[7,4,16,128]{3,2,1,0:T(8,128)S(1)}, f32[7,4,16,128]{3,2,1,0:T(8,128)S(1)}, u32[]{:S(2)}, u32[]{:S(2)}) collective-permute-start(f32[7,4,16,128]{3,2,1,0:T(8,128)S(1)} %get-tuple-element.16), channel_id=1, source_target_pairs={{0,1},{1,0},{2,3},{3,2},{4,5},{5,4},{6,7},{7,6},{8,9},{9,8},{10,11... | collective-permute-start | bytes 688136 | tf_op jit(solution)/shard_map/ppermute | solution.py:142
